TPU v7x, 128 devices: a whole 4x4x4 slice. The times are simulated.
128 devices in a mesh: sect: 2 (over core), dev: 64 (over x, y, z).
Axes of the slice: x: 4, y: 4, z: 4, core: 2. Of those that a mesh axis runs over, the one named last changes fastest.
Arguments:
- atmosphere_state: bfloat16 [4, 72, 131072], P(None, None, ('sect', 'dev')), may hold values from -5 to 5
- metric: float32 [2, 131072], P(None, ('sect', 'dev')), may hold values from 0.05 to 0.5
- column_group_target: int32 [131072, 1], replicated, may hold values from 0 to 127; in each aligned block of 1024 rows (0 to 1023, 1024 to 2047, ...) at most 16 rows name the same one
- physics_input_layer: bfloat16 [288, 1024], replicated, may hold values from -0.375 to 0.375
- physics_tendency_layer: bfloat16 [1024, 288], replicated, may hold values from -0.1875 to 0.1875
- physics_flux_layer: bfloat16 [1024, 4], replicated, may hold values from -0.1875 to 0.1875
- block_to_tile: int32 [1024], replicated, may hold values from 0 to 1023, as said below
- remap_weight_matrix: float32 [128, 128], replicated, may hold values from -0.5 to 0.5
- ocean_land_mask: int32 [1024, 128], P(('sect', 'dev')), may hold values 0 or 1
- ocean_sea_anomaly: float32 [1024, 128], P(('sect', 'dev')), may hold values from -5 to 5
- flux_sea_response: float32 [4], replicated, may hold values from -3 to 3
Outputs:
- stepped_state: bfloat16 [4, 72, 131072], P(None, None, ('sect', 'dev'))
- group_layout_tendency: bfloat16 [262144, 288], P(('sect', 'dev'))
- updated_sea_temp: float32 [1024, 128], P(('sect', 'dev'))
- atmosphere_sea_temp: float32 [131072], P(('sect', 'dev'))
Inputs may be any that keep to these rules, and one draw needn't show every extreme that they name: `column_group_target`: among the columns of one device no group is named more than 16 times; in some devices one group is named exactly 16 times. `block_to_tile`: A permutation: block j of device a (block a 8 + j) feeds tile j of device (a + s_j) mod the number of devices, with shifts s_j common to all devices; at most 2 of the shifts are equal, and exactly 2 are equal in every draw.
All inputs are finite; a program needn't handle non-finite values. No bound on the sum of `ocean_land_mask` on one device may be relied on, other than what follows from the above.
Results may differ from a plain program's by a relative error of at most 0.0068.
Values may be sent and summed in bfloat16 or wider, within the bound.
A program may use at most 128 MiB of HBM per device.

v0:
```python
import jax
import jax.numpy as jnp
import numpy as np
from jax import lax
from jax.sharding import PartitionSpec as P

BLOCK_CELLS = 128


def gll_tables():
    gll_nodes = np.array([-1.0, -1.0 / np.sqrt(5.0), 1.0 / np.sqrt(5.0), 1.0])
    offdiag = gll_nodes[:, None] - gll_nodes[None, :] + np.eye(4)
    bary = np.prod(offdiag, axis=1)
    derivative = bary[:, None] / (bary[None, :] * offdiag)
    diag_sum = np.sum(1.0 / offdiag - np.eye(4), axis=1)
    derivative = derivative * (1.0 - np.eye(4)) + np.eye(4) * diag_sum[:, None]
    first_dir = np.kron(np.eye(8), np.kron(np.eye(4), derivative)).T
    second_dir = np.kron(np.eye(8), np.kron(derivative, np.eye(4))).T
    return (
        jnp.asarray(first_dir, jnp.float32).astype(jnp.bfloat16),
        jnp.asarray(second_dir, jnp.float32).astype(jnp.bfloat16),
    )


def dynamics(atmosphere_state, metric):
    first_dir, second_dir = gll_tables()
    array_shape = atmosphere_state.shape
    flat = atmosphere_state.reshape(-1, 128)
    grad_first = jnp.dot(flat, first_dir, preferred_element_type=jnp.float32).reshape(array_shape)
    grad_second = jnp.dot(flat, second_dir, preferred_element_type=jnp.float32).reshape(array_shape)
    wind_first = (atmosphere_state[0].astype(jnp.float32) * metric[0][None, :])[None]
    wind_second = (atmosphere_state[1].astype(jnp.float32) * metric[1][None, :])[None]
    advected = (
        atmosphere_state.astype(jnp.float32) - wind_first * grad_first - wind_second * grad_second
    )
    return advected.astype(jnp.bfloat16)


def relay(outgoing, work):
    return work(lax.all_to_all(outgoing, ("sect", "dev"), split_axis=0, concat_axis=0, tiled=True))


def per_device(
    atmosphere_state,
    metric,
    column_group_target,
    physics_input_layer,
    physics_tendency_layer,
    physics_flux_layer,
    block_to_tile,
    remap_weight_matrix,
    ocean_land_mask,
    ocean_sea_anomaly,
    flux_sea_response,
):
    devices = lax.axis_size(("sect", "dev"))
    myself = lax.axis_index(("sect", "dev"))
    nfields, vertical_levels, cols_dev = atmosphere_state.shape
    col_width = nfields * vertical_levels
    nflux = physics_flux_layer.shape[1]
    capacity = 2 * cols_dev // devices
    blocks_per_group = ocean_sea_anomaly.shape[0]
    advected = dynamics(atmosphere_state, metric)
    columns = advected.reshape(col_width, cols_dev).T
    all_targets = column_group_target[:, 0].reshape(devices, cols_dev)
    my_targets = lax.dynamic_index_in_dim(all_targets, myself, 0, keepdims=False)
    onehot = (my_targets[:, None] == jnp.arange(devices, dtype=jnp.int32)[None, :]).astype(
        jnp.int32
    )
    position = jnp.sum((jnp.cumsum(onehot, axis=0) - onehot) * onehot, axis=1)
    slot_index = my_targets * capacity + position

    def physics(slot_block):
        lead, count = (slot_block.shape[0], slot_block.shape[1])
        flat = slot_block.reshape(-1, col_width)
        hidden = jax.nn.silu(
            jnp.dot(flat, physics_input_layer, preferred_element_type=jnp.float32)
        ).astype(jnp.bfloat16)
        tendency = jnp.dot(hidden, physics_tendency_layer, preferred_element_type=jnp.float32)
        updated = (flat.astype(jnp.float32) + tendency).astype(jnp.bfloat16)
        fluxes = jnp.dot(hidden, physics_flux_layer, preferred_element_type=jnp.float32).astype(
            jnp.bfloat16
        )
        return (
            updated.reshape(lead, count, col_width),
            tendency.astype(jnp.bfloat16).reshape(lead, count, col_width),
            fluxes.reshape(lead, count, nflux),
        )

    outgoing = jnp.zeros((devices * capacity, col_width), jnp.bfloat16).at[slot_index].set(columns)
    outgoing = outgoing.reshape(devices, capacity, col_width)
    incoming = jnp.sum((all_targets == myself).astype(jnp.int32), axis=1)
    occupied = jnp.arange(capacity, dtype=jnp.int32)[None, :] < incoming[:, None]
    updated, tendency, fluxes = relay(outgoing, physics)
    group_layout_tendency = jnp.where(
        occupied[:, :, None], tendency, jnp.zeros_like(tendency)
    ).reshape(devices * capacity, col_width)
    back_cols, back_flux = (
        lax.all_to_all(updated, ("sect", "dev"), split_axis=0, concat_axis=0, tiled=True),
        lax.all_to_all(fluxes, ("sect", "dev"), split_axis=0, concat_axis=0, tiled=True),
    )
    new_columns = back_cols.reshape(devices * capacity, col_width)[slot_index]
    col_flux = back_flux.reshape(devices * capacity, nflux)[slot_index].T
    stepped_state = new_columns.T.reshape(nfields, vertical_levels, cols_dev)
    tile_table = block_to_tile.reshape(devices, blocks_per_group)
    total_blocks = devices * blocks_per_group
    inverse = (
        jnp.zeros((total_blocks,), jnp.int32)
        .at[block_to_tile]
        .set(jnp.arange(total_blocks, dtype=jnp.int32))
    )
    source = lax.dynamic_slice_in_dim(inverse, myself * blocks_per_group, blocks_per_group)
    local_tiles = lax.dynamic_index_in_dim(tile_table, myself, 0, keepdims=False)
    every_flux = lax.all_gather(col_flux, ("sect", "dev"), axis=1, tiled=True)
    picked = every_flux.reshape(nflux, total_blocks, BLOCK_CELLS)[:, source]
    mask_as_float = ocean_land_mask.astype(jnp.float32)
    cell_surface_flux = mask_as_float[None] * jnp.einsum(
        "im,ktm->kti",
        remap_weight_matrix,
        picked.astype(jnp.float32),
        precision=lax.Precision.HIGHEST,
    )
    updated_sea_temp = ocean_sea_anomaly + jnp.einsum(
        "l,leu->eu", flux_sea_response, cell_surface_flux, precision=lax.Precision.HIGHEST
    )
    ocean_cell_sea_temp = mask_as_float * updated_sea_temp
    every_sea_temp = lax.all_gather(ocean_cell_sea_temp, ("sect", "dev"), axis=0, tiled=True)
    returned_rows = every_sea_temp[local_tiles]
    atmosphere_sea_temp = jnp.einsum(
        "xn,kx->kn", remap_weight_matrix, returned_rows, precision=lax.Precision.HIGHEST
    ).reshape(cols_dev)
    return (stepped_state, group_layout_tendency, updated_sea_temp, atmosphere_sea_temp)


def solution(mesh):
    placed = (
        P(None, None, ("sect", "dev")),
        P(None, ("sect", "dev")),
        P(),
        P(),
        P(),
        P(),
        P(),
        P(),
        P(("sect", "dev"), None),
        P(("sect", "dev"), None),
        P(),
    )
    return jax.shard_map(
        per_device,
        mesh=mesh,
        in_specs=placed,
        out_specs=(
            P(None, None, ("sect", "dev")),
            P(("sect", "dev"), None),
            P(("sect", "dev"), None),
            P(("sect", "dev")),
        ),
        check_vma=False,
    )
```

profile of v0, /device:TPU:1, one launch (start us, length us, event | category | flops | bytes accessed | tf_op | source)
XLA Modules:
  0.0 556.8 jit_solution(15177612598236941821)
XLA Ops:
  7.2 0.0 copy-start
  7.2 0.5 broadcast.137
  7.7 2.9 reduce.3
  10.6 0.1 reshape_squeeze.3
  10.7 0.0 copy-start.8
  10.8 0.1 copy.44
  10.9 0.0 copy-start.6
  10.9 0.2 fusion.5
  11.2 0.0 copy-start.11
  11.2 0.1 copy.45
  11.3 0.4 fusion.4
  11.7 0.0 copy-done.8
  11.7 0.3 copy-done.6
  12.0 0.3 reshape.161
  12.3 0.0 copy-done.11
  12.3 0.3 convolution_bitcast_fusion.1
  12.6 0.4 copy.46
  13.0 1.2 reshape.162
  14.2 1.1 convolution_bitcast_fusion
  15.3 0.4 copy.47
  15.6 0.0 copy-start.7
  15.7 0.0 copy-start.5
  15.7 1.2 reshape.163
  16.9 0.1 multiply_bitcast_fusion.1
  16.9 0.6 copy-done.5
  17.5 1.7 subtract_convert_fusion
  19.2 0.4 copy.48
  19.6 5.5 scatter_custom_fusion
  25.1 34.2 %all_to_all.15 = bf16[128,16,288]{2,1,0:T(8,128)(2,1)S(1)} all-to-all(bf16[128,16,288]{2,1,0:T(8,128)(2,1)S(1)} %bitcast.77), channel_id=1, replica_groups=mesh['sect'=2,'dev'=64] {'sect','dev'}, dimensions={0} | all-to-all | bytes 2359296 | tf_op jit(solution)/shard_map/all_to_all | solution.py:40
  59.3 3.4 multiply_convert_fusion
  62.7 2.1 copy-done.2
  64.7 1.2 convolution_convert_fusion
  65.9 0.2 reshape.170
  66.1 0.8 copy.53
  66.8 6.2 %all-to-all-start.2 = ((bf16[128,16,4]{1,2,0:T(4,128)(2,1)}), bf16[128,16,4]{1,2,0:T(4,128)(2,1)S(1)}, u32[]{:S(2)}, u32[]{:S(2)}) async-start(bf16[128,16,4]{1,2,0:T(4,128)(2,1)} %copy.53), calls=%async_computation.2 | async-start | bytes 262144 | tf_op jit(solution)/shard_map/all_to_all | solution.py:100
  73.0 0.0 all-gather.2.cloned.1.call-start
  73.1 0.0 copy-start.9
  73.1 9.7 %all-to-all-done.2 = bf16[128,16,4]{1,2,0:T(4,128)(2,1)S(1)} async-done(((bf16[128,16,4]{1,2,0:T(4,128)(2,1)}), bf16[128,16,4]{1,2,0:T(4,128)(2,1)S(1)}, u32[]{:S(2)}, u32[]{:S(2)}) %all-to-all-start.2) | async-done | bytes 16416 | tf_op jit(solution)/shard_map/all_to_all | solution.py:100
  82.8 0.8 copy.54
  83.7 4.3 gather_fusion.1
  88.0 0.0 all-gather.2.cloned.1.call-update
  88.0 0.1 convert_reduce_fusion
  88.2 0.1 iota_compare_fusion.3
  88.3 0.1 lt.62
  88.4 0.1 reshape.173
  88.5 1.5 copy.50
  90.0 4.1 add_convert_fusion
  94.1 1.6 copy.51
  95.7 4.3 all-to-all-start.1
  100.1 4.3 scatter_custom_fusion.1
  104.4 0.1 compare_select_fusion.3
  104.5 1.1 convert_select_fusion
  105.6 18.6 %all-to-all-done.1 = bf16[128,16,288]{2,1,0:T(8,128)(2,1)S(1)} async-done(((bf16[128,16,288]{2,1,0:T(8,128)(2,1)}), bf16[128,16,288]{2,1,0:T(8,128)(2,1)S(1)}, u32[]{:S(2)}, u32[]{:S(2)}) %all-to-all-start.1) | async-done | bytes 1179680 | tf_op jit(solution)/shard_map/all_to_all | solution.py:99
  124.2 3.9 gather_fusion
  128.1 1.1 copy.52
  129.2 76.3 %all-gather.2.cloned.1.call-done = bf16[4,131072]{0,1:T(8,128)(2,1)} async-done(((bf16[4,1024]{0,1:T(8,128)(2,1)}), bf16[4,131072]{0,1:T(8,128)(2,1)}) %all-gather.2.cloned.1.call-update) | async-done | bytes 1048592 | tf_op jit(solution)/shard_map/all_gather | solution.py:114
  205.5 24.1 %copy.55 = bf16[4,1024,128]{2,0,1:T(4,128)(2,1)S(1)} copy(bf16[4,1024,128]{0,2,1:T(8,128)(2,1)} %bitcast.75) | data formatting | bytes 2097152 | tf_op jit(solution)/shard_map/reshape | solution.py:115
  229.6 0.6 gather_fusion.2
  230.1 0.2 convolution_multiply_fusion
  230.3 0.2 fusion.13
  230.5 0.6 convert_multiply_fusion
  231.1 317.5 %all_gather.7 = f32[1024,128]{1,0:T(8,128)S(1)} all-gather(f32[8,128]{1,0:T(8,128)S(1)} %get-tuple-element.8), channel_id=1, replica_groups=mesh['sect'=2,'dev'=64] {'sect','dev'}, dimensions={0}, use_global_device_ids=true | all-gather | bytes 528384 | tf_op jit(solution)/shard_map/all_gather | solution.py:127
  548.7 0.6 gather_fusion.3
  549.2 0.8 convolution_bitcast_fusion.2
  (38 shorter events, 0.2 us)
Async XLA Ops:
  7.2 52.1 %copy-start = (bf16[288,1024]{1,0:T(8,128)(2,1)S(1)}, bf16[288,1024]{1,0:T(8,128)(2,1)}, u32[]{:S(2)}) copy-start(bf16[288,1024]{1,0:T(8,128)(2,1)} %param.16) | copy-start | bytes 1769476
  10.7 0.9 copy-start.8
  10.9 0.8 copy-start.15
  10.9 1.1 copy-start.6
  11.2 1.1 copy-start.11
  15.6 1.2 copy-start.7
  15.7 1.9 copy-start.5
  59.3 3.4 copy-start.3
  59.3 5.5 copy-start.14
  62.7 2.1 copy-start.2
  66.8 16.0 %all-to-all-start.2 = ((bf16[128,16,4]{1,2,0:T(4,128)(2,1)}), bf16[128,16,4]{1,2,0:T(4,128)(2,1)S(1)}, u32[]{:S(2)}, u32[]{:S(2)}) async-start(bf16[128,16,4]{1,2,0:T(4,128)(2,1)} %copy.53), calls=%async_computation.2 | async-start | bytes 262144 | tf_op jit(solution)/shard_map/all_to_all | solution.py:100
  73.0 132.4 %all-gather.2.cloned.1.call-start = ((), (), s32[]{:S(2)}) async-start(), calls=%async_computation.3 | async-start | bytes 33816576 | tf_op jit(solution)/shard_map/all_gather | solution.py:114
  73.1 15.0 %copy-start.9 = (s32[128,1024]{1,0:T(8,128)S(1)}, s32[128,1024]{1,0:T(8,128)}, u32[]{:S(2)}) copy-start(s32[128,1024]{1,0:T(8,128)} %copy-done.8) | copy-start | bytes 1572868
  83.7 4.7 copy-start.13
  83.7 4.7 copy-start.12
  83.7 4.8 copy-start.4
  95.7 28.4 %all-to-all-start.1 = ((bf16[128,16,288]{2,1,0:T(8,128)(2,1)}), bf16[128,16,288]{2,1,0:T(8,128)(2,1)S(1)}, u32[]{:S(2)}, u32[]{:S(2)}) async-start(bf16[128,16,288]{2,1,0:T(8,128)(2,1)} %bitcast.80), calls=%async_computation.1 | async-start | bytes 3145728 | tf_op jit(solution)/shard_map/all_to_all | solution.py:99
  205.4 24.7 %copy-start.10 = (f32[128,128]{1,0:T(8,128)S(1)}, f32[128,128]{1,0:T(8,128)}, u32[]{:S(2)}) copy-start(f32[128,128]{1,0:T(8,128)} %param.20) | copy-start | bytes 196612
  205.5 24.9 %copy-start.17 = (f32[4]{0:T(128)S(1)}, f32[4]{0:T(128)}, u32[]{:S(2)}) copy-start(f32[4]{0:T(128)} %param.23) | copy-start | bytes 52
  205.5 25.1 %copy-start.16 = (f32[8,128]{1,0:T(8,128)S(1)}, f32[8,128]{1,0:T(8,128)}, u32[]{:S(2)}) copy-start(f32[8,128]{1,0:T(8,128)} %param.22) | copy-start | bytes 12292
  205.5 344.5 %copy-start.1 = (bf16[288,1024]{1,0:T(8,128)(2,1)S(1)}, bf16[288,1024]{1,0:T(8,128)(2,1)}, u32[]{:S(2)}) copy-start(bf16[288,1024]{1,0:T(8,128)(2,1)} %param.16) | copy-start | bytes 1769476
Sparse Core Ops, SparseCore 0:
  88.1 117.2 all-gather.1
where the time goes:
time: 558 us; the launch traced here: 557 us
  blocking collectives  352 us (63%)
  waiting for transfers between devices  105 us (19%)
  local copies, waits for them, and re-layouts  57 us (10%)
  between operations  14.5 us (3%)
  matrix products  11.2 us (2%)
  starting transfers between devices  10.5 us (2%)
  other arithmetic  7.34 us (1%)
    all_gather x1, blocking collectives, per_device(): lax.all_gather(ocean_cell_sea_temp, ('sect', 'dev'), axis=0, tiled=True)  318 us
    all_gather x1, waiting for transfers between devices, per_device(): every_flux = lax.all_gather(col_flux, ('sect', 'dev'), axis=1, tiled=True)  76.3 us
    all_to_all x1, blocking collectives, relay(): lax.all_to_all(outgoing, ('sect', 'dev'), split_axis=0, concat_axis=0, ti...  34.2 us
    reshape x1, local copies, waits for them, and re-layouts, per_device(): picked = every_flux.reshape(nflux, total_blocks, BLOCK_CELLS)[:, source]  24.1 us
    all_to_all x1, waiting for transfers between devices, per_device(): lax.all_to_all(updated, ('sect', 'dev'), split_axis=0, concat_axis=0, til...  18.6 us
  transfers between devices with their start and end apart: 3, of which 3 were waited for; matrix products, arithmetic and copies ran while one was open for 3% of the time, Pallas kernels for 0%

commit v1 on v0

v1 whole, which is shorter than its diff:
```python
import functools
import itertools
import random

import jax
import jax.numpy as jnp
import numpy as np
from jax import lax
from jax.experimental import pallas as pl
from jax.experimental.pallas import tpu as pltpu
from jax.sharding import PartitionSpec as P

MESH = pl.DeviceIdType.MESH
BF16 = jnp.bfloat16
F32 = jnp.float32
I32 = jnp.int32

DEVICES = 128
CAP = 16
COLS = 1024
WIDTH = 288
HID = 1024
ROWS = 40
STEP = 256
PART = 512
NT = (((1,), (1,)), ((), ()))


def gll_tables():
    gll_nodes = np.array([-1.0, -1.0 / np.sqrt(5.0), 1.0 / np.sqrt(5.0), 1.0])
    offdiag = gll_nodes[:, None] - gll_nodes[None, :] + np.eye(4)
    bary = np.prod(offdiag, axis=1)
    derivative = bary[:, None] / (bary[None, :] * offdiag)
    diag_sum = np.sum(1.0 / offdiag - np.eye(4), axis=1)
    derivative = derivative * (1.0 - np.eye(4)) + np.eye(4) * diag_sum[:, None]
    first_dir = np.kron(np.eye(8), np.kron(np.eye(4), derivative)).T
    second_dir = np.kron(np.eye(8), np.kron(derivative, np.eye(4))).T
    both = np.concatenate([first_dir, second_dir], axis=1)
    return jnp.asarray(both, F32).astype(BF16)


def message_order():
    hops = lambda k: min(k, 4 - k)
    offsets = list(itertools.product(range(2), range(4), range(4), range(4)))
    random.Random(1).shuffle(offsets)
    offsets.sort(key=lambda o: (-sum(hops(k) for k in o[1:]), o == (0, 0, 0, 0)))
    here = offsets.index((0, 0, 0, 0))
    offsets.append(offsets.pop(here))
    return offsets


ORDER = message_order()


def device(index):
    return (lax.div(index, 64), lax.rem(index, 64))


def dot(a, b):
    return jnp.dot(a, b, preferred_element_type=F32)


def dot_nt(a, b, precision=None):
    return lax.dot_general(a, b, NT, precision=precision, preferred_element_type=F32)


def iota(shape, dim):
    return lax.broadcasted_iota(I32, shape, dim)


def one_hot(condition):
    return jnp.where(condition, 1.0, 0.0).astype(BF16)


def kernel(
    state_hbm,
    target_hbm,
    w1_hbm,
    w2t_hbm,
    metric_ref,
    w3t_ref,
    tile_ref,
    remap_ref,
    mask_ref,
    anomaly_ref,
    response_ref,
    deriv_ref,
    order_ref,
    stepped_hbm,
    layout_hbm,
    updated_ref,
    atmos_ref,
    x_v,
    target_v,
    w1_v,
    w1t_v,
    w23_v,
    adv_v,
    hid_v,
    tend_v,
    step_v,
    lay_v,
    q_v,
    send_v,
    recv_v,
    near_send,
    near_recv,
    far_send,
    far_recv,
    in_sem,
    out_sem,
    lay_sem,
    send_sem,
    recv_sem,
    near_sem,
    far_sem,
):
    core, chip = lax.axis_index("sect"), lax.axis_index("dev")
    me = core * 64 + chip
    high, low = lax.div(me, 8), lax.rem(me, 8)

    loads = [
        pltpu.make_async_copy(target_hbm.at[me], target_v, in_sem.at[0]),
        pltpu.make_async_copy(w1_hbm, w1_v, in_sem.at[1]),
        pltpu.make_async_copy(state_hbm, x_v, in_sem.at[2]),
        pltpu.make_async_copy(w2t_hbm, w23_v.at[pl.ds(0, WIDTH)], in_sem.at[3]),
    ]
    for load in loads:
        load.start()

    barrier = pltpu.get_barrier_semaphore()

    @pl.loop(1, DEVICES, unroll=4)
    def _(i):
        pl.semaphore_signal(
            barrier, inc=1, device_id=device(lax.rem(me + 64 + i + lax.div(i, 64), DEVICES)), device_id_type=MESH
        )

    lane, sub = iota((8, 128), 1), iota((8, 128), 0)
    tile8 = tile_ref[0:1, :]
    shift_row = jnp.where(iota((1, 128), 1) < 8, tile8 >> 3, -1)
    shift_col = jnp.sum(jnp.where(lane == sub, shift_row, 0), axis=1, keepdims=True)
    same = jnp.where((shift_row == shift_col) & (lane < 8), 1, 0)
    twin_row = jnp.sum(jnp.where(sub < lane, same, 0), axis=0, keepdims=True)
    twin_col = jnp.sum(jnp.where(lane < sub, same, 0), axis=1, keepdims=True)

    order = order_ref[...]
    x, y, z = lax.div(chip, 16), lax.rem(lax.div(chip, 4), 4), lax.rem(chip, 4)
    to_device = (
        ((order[:, 0:1] + core) & 1) * 64
        + ((order[:, 1:2] + x) & 3) * 16
        + ((order[:, 2:3] + y) & 3) * 4
        + ((order[:, 3:4] + z) & 3)
    )

    loads[0].wait()
    targets = jnp.concatenate([target_v[k : k + 1, :] for k in range(8)], axis=1)
    before = one_hot(iota((STEP, STEP), 0) < iota((STEP, STEP), 1))
    message = iota((DEVICES, STEP), 0)
    taken = jnp.zeros((DEVICES, 1), F32)
    slots = []
    for c in range(COLS // STEP):
        hit = to_device == targets[:, c * STEP : (c + 1) * STEP]
        hits = jnp.where(hit, 1.0, 0.0)
        earlier = dot(hits.astype(BF16), before) + taken
        taken = taken + jnp.sum(hits, axis=1, keepdims=True)
        slot = jnp.where(hit, earlier.astype(I32) + CAP * message, 0)
        slots.append(jnp.sum(slot, axis=0, keepdims=True))
    slots = jnp.concatenate(slots, axis=1)

    ocean = mask_ref[...].astype(F32)
    ahead = jnp.concatenate([ocean, ocean * anomaly_ref[...]], axis=0).astype(BF16)
    near_send[...] = ahead
    near_recv[low] = ahead

    loads[1].wait()
    unit = one_hot(iota((256, 256), 0) == iota((256, 256), 1))
    for b in range(HID // 256):
        rows = slice(b * 256, (b + 1) * 256)
        w1t_v[rows, :] = dot_nt(unit, w1_v[:, rows]).astype(BF16)
    loads[3].wait()
    w23_v[WIDTH : WIDTH + 16, :] = jnp.concatenate([w3t_ref[...].astype(F32), jnp.zeros((12, HID), F32)], axis=0).astype(BF16)

    loads[2].wait()
    deriv = deriv_ref[...]
    stores = []
    for c in range(COLS // STEP):
        for b in range(STEP // 128):
            at = slice(c * STEP + b * 128, c * STEP + (b + 1) * 128)
            field = x_v[:, at]
            grads = dot(field, deriv)
            wide = field.astype(F32)
            wind_first = wide[0:72] * metric_ref[0:1, at]
            wind_second = wide[72:144] * metric_ref[1:2, at]
            moved = (
                wide
                - jnp.concatenate([wind_first] * 4, axis=0) * grads[:, 0:128]
                - jnp.concatenate([wind_second] * 4, axis=0) * grads[:, 128:256]
            )
            adv_v[:, at] = moved.astype(BF16)
        at = slice(c * STEP, (c + 1) * STEP)
        column = adv_v[:, at]
        for b in range(HID // 256):
            rows = slice(b * 256, (b + 1) * 256)
            pre = dot(w1t_v[rows, :], column)
            hid_v[rows, at] = (0.5 * pre * (1.0 + jnp.tanh(0.5 * pre))).astype(BF16)
        result = dot(w23_v[...], hid_v[:, at])
        tendency = result[0:WIDTH]
        step_v[:, at] = (column.astype(F32) + tendency).astype(BF16)
        tendency = tendency.astype(BF16)
        tend_v[0:WIDTH, at] = tendency
        for g in range(1, 4):
            tend_v[256 + 32 * g : 288 + 32 * g, at] = tendency[256:288]
        flux = result[WIDTH : WIDTH + 8].astype(BF16).astype(F32)
        mixed = sum(response_ref[k] * flux[k : k + 1] for k in range(4))
        for b in range(STEP // 128):
            j = c * (STEP // 128) + b
            q_v[j : j + 1, :] = mixed[:, b * 128 : (b + 1) * 128]
        store = pltpu.make_async_copy(step_v.at[:, at], stepped_hbm.at[:, at], out_sem.at[c])
        store.start()
        stores.append(store)

    q = q_v[...]
    q_rows = jnp.concatenate([q, jnp.zeros((120, 128), F32)], axis=0).astype(BF16)
    flux_to = jnp.where(shift_row < 0, -1, (shift_row + me) & (DEVICES - 1))
    flux_rows = [dot(one_hot((to_device == flux_to) & (twin_row == u)), q_rows) for u in range(2)]

    pl.semaphore_wait(barrier, DEVICES - 1)

    @pl.loop(1, 8)
    def _(i):
        peer = high * 8 + lax.rem(low + i, 8)
        pltpu.make_async_remote_copy(
            near_send, near_recv.at[low], near_sem.at[0], near_sem.at[1], device_id=device(peer), device_id_type=MESH
        ).start()

    cores = [lax.rem(core + k, 2) for k in range(2)]
    xs = [lax.rem(x + k, 4) * 16 for k in range(4)]
    ys = [lax.rem(y + k, 4) * 4 for k in range(4)]
    zs = [lax.rem(z + k, 4) for k in range(4)]
    here = pltpu.make_async_copy(send_v.at[DEVICES - 1], recv_v.at[me], recv_sem.at[high])
    packed_row = iota((PART // CAP, 8, 128), 1)
    keep = (iota((PART, 128), 0) & 15) >> 2 == iota((PART, 128), 1) >> 5
    for k in range(DEVICES * CAP // PART):
        pick = one_hot(iota((PART, COLS), 0) + k * PART == slots)
        placed = dot_nt(pick, tend_v[...])
        first, count = k * PART // CAP, PART // CAP
        into = pl.ds(first, count)
        main = placed[:, 0:256].astype(BF16)
        send_v[into, 0:16, :] = main[:, 0:128].reshape(count, CAP, 128)
        send_v[into, 16:32, :] = main[:, 128:256].reshape(count, CAP, 128)
        tail = jnp.where(keep, placed[:, 256:384], 0.0).reshape(count, CAP, 128)
        tail = tail[:, 0:8] + tail[:, 8:16]
        tail = tail + jnp.concatenate([tail[:, 4:8], tail[:, 0:4]], axis=1)
        for u in range(2):
            row = flux_rows[u][first : first + count].reshape(count, 1, 128)
            tail = jnp.where(packed_row == 4 + u, row, tail)
        send_v[into, 32:40, :] = tail.astype(BF16)
        for i in range(first, first + count):
            if i == DEVICES - 1:
                here.start()
                continue
            a, b, e, f = ORDER[i]
            pltpu.make_async_remote_copy(
                send_v.at[i],
                recv_v.at[me],
                send_sem,
                recv_sem.at[high],
                device_id=(cores[a], xs[b] + ys[e] + zs[f]),
                device_id_type=MESH,
            ).start()
        if k == 1:
            got = near_recv.at[pl.ds(0, 7)]
            pltpu.make_async_copy(got, got, near_sem.at[1]).wait()
            source = (low + shift_col) & 7
            source = jnp.concatenate([source, source], axis=0)
            chosen = jnp.zeros((16, 128), F32)
            for l in range(8):
                chosen = chosen + jnp.where(source == l, near_recv[l].astype(F32), 0.0)
            chosen = chosen.astype(BF16)
            far_send[...] = chosen
            far_recv[high] = chosen

            @pl.loop(1, 16)
            def _(i):
                peer = lax.rem(high + i, 16) * 8 + low
                pltpu.make_async_remote_copy(
                    far_send, far_recv.at[high], far_sem.at[0], far_sem.at[1], device_id=device(peer), device_id_type=MESH
                ).start()

    got = far_recv.at[pl.ds(0, 15)]
    pltpu.make_async_copy(got, got, far_sem.at[1]).wait()
    source = ((me + shift_col) & (DEVICES - 1)) >> 3
    source = jnp.concatenate([source, source], axis=0)
    chosen = jnp.zeros((16, 128), F32)
    for h in range(16):
        chosen = chosen + jnp.where(source == h, far_recv[h].astype(F32), 0.0)
    remap = remap_ref[...]
    cell = dot_nt(q, remap, lax.Precision.HIGHEST)
    masked = chosen[8:16] + chosen[0:8] * cell
    atmos_ref[...] = jnp.dot(masked, remap, precision=lax.Precision.HIGHEST, preferred_element_type=F32)

    unit = one_hot(iota((128, 128), 0) == iota((128, 128), 1))
    slot, row = iota((128, 64), 0), iota((128, 64), 1)
    spread = one_hot((row >> 3 == slot >> 4) & ((row & 7) == (slot & 3)))
    held = (iota((128, 128), 0) & 15) >> 2 == iota((128, 128), 1) >> 5
    fold = one_hot(iota((32, 128), 0) == (iota((32, 128), 1) & 31))
    flux_row = ((me - shift_col) & (DEVICES - 1)) * 8 + 4 + twin_col
    q_v[...] = jnp.zeros((8, 128), F32)

    @pl.loop(0, 16)
    def _(n):
        group = lax.rem(high + 8 + n, 16)
        eight = pl.ds(pl.multiple_of(group * 8, 8), 8)
        got = recv_v.at[eight]
        pltpu.make_async_copy(got, got, recv_sem.at[group]).wait()
        lanes = pl.ds(pl.multiple_of(group * 128, 128), 128)
        for half in range(2):
            part = recv_v[eight, 16 * half : 16 * half + 16, :].reshape(128, 128)
            lay_v[128 * half : 128 * half + 128, lanes] = dot_nt(unit, part).astype(BF16)
        packed = recv_v[eight, 32:40, :].astype(F32).reshape(64, 128).astype(BF16)
        wide = jnp.where(held, dot(spread, packed), 0.0).astype(BF16)
        lay_v[256:288, lanes] = dot_nt(fold, wide).astype(BF16)
        q_v[...] += dot(one_hot(iota((8, 64), 1) + group * 64 == flux_row), packed)
        pltpu.make_async_copy(lay_v.at[:, lanes], layout_hbm.at[:, lanes], lay_sem).start()

    cell = dot_nt(q_v[...], remap, lax.Precision.HIGHEST)
    updated_ref[...] = anomaly_ref[...] + mask_ref[...].astype(F32) * cell

    for store in stores:
        store.wait()
    pltpu.make_async_copy(lay_v, layout_hbm, lay_sem).wait()
    sent = send_v.at[pl.ds(0, DEVICES - 1)]
    pltpu.make_async_copy(sent, sent, send_sem).wait()
    sent = near_recv.at[pl.ds(0, 7)]
    pltpu.make_async_copy(sent, sent, near_sem.at[0]).wait()
    sent = far_recv.at[pl.ds(0, 15)]
    pltpu.make_async_copy(sent, sent, far_sem.at[0]).wait()


def per_device(
    atmosphere_state,
    metric,
    column_group_target,
    physics_input_layer,
    physics_tendency_layer,
    physics_flux_layer,
    block_to_tile,
    remap_weight_matrix,
    ocean_land_mask,
    ocean_sea_anomaly,
    flux_sea_response,
):
    anywhere, vmem = pl.BlockSpec(memory_space=pl.ANY), pl.BlockSpec(memory_space=pltpu.VMEM)
    smem = pl.BlockSpec(memory_space=pltpu.SMEM)
    order = np.zeros((DEVICES, 8), np.int32)
    order[:, :4] = ORDER
    stepped, layout, updated, atmos = pl.pallas_call(
        kernel,
        out_shape=[
            jax.ShapeDtypeStruct((WIDTH, COLS), BF16),
            jax.ShapeDtypeStruct((WIDTH, DEVICES * CAP), BF16),
            jax.ShapeDtypeStruct((8, 128), F32),
            jax.ShapeDtypeStruct((8, 128), F32),
        ],
        in_specs=[anywhere] * 4 + [vmem] * 6 + [smem] + [vmem] * 2,
        out_specs=[anywhere, anywhere, vmem, vmem],
        scratch_shapes=[
            pltpu.VMEM((WIDTH, COLS), BF16),
            pltpu.VMEM((8, 128), I32),
            pltpu.VMEM((WIDTH, HID), BF16),
            pltpu.VMEM((HID, WIDTH), BF16),
            pltpu.VMEM((WIDTH + 16, HID), BF16),
            pltpu.VMEM((WIDTH, COLS), BF16),
            pltpu.VMEM((HID, COLS), BF16),
            pltpu.VMEM((384, COLS), BF16),
            pltpu.VMEM((WIDTH, COLS), BF16),
            pltpu.VMEM((WIDTH, DEVICES * CAP), BF16),
            pltpu.VMEM((8, 128), F32),
            pltpu.VMEM((DEVICES, ROWS, 128), BF16),
            pltpu.VMEM((DEVICES, ROWS, 128), BF16),
            pltpu.VMEM((16, 128), BF16),
            pltpu.VMEM((8, 16, 128), BF16),
            pltpu.VMEM((16, 128), BF16),
            pltpu.VMEM((16, 16, 128), BF16),
            pltpu.SemaphoreType.DMA((4,)),
            pltpu.SemaphoreType.DMA((COLS // STEP,)),
            pltpu.SemaphoreType.DMA,
            pltpu.SemaphoreType.DMA,
            pltpu.SemaphoreType.DMA((16,)),
            pltpu.SemaphoreType.DMA((2,)),
            pltpu.SemaphoreType.DMA((2,)),
        ],
        compiler_params=pltpu.CompilerParams(
            collective_id=0, has_side_effects=True, vmem_limit_bytes=48 * 1024 * 1024
        ),
        name="coupling_interval",
    )(
        atmosphere_state.reshape(WIDTH, COLS),
        column_group_target.reshape(DEVICES, 8, 128),
        physics_input_layer,
        physics_tendency_layer.T,
        metric,
        physics_flux_layer.T,
        block_to_tile.reshape(8, 128),
        remap_weight_matrix,
        ocean_land_mask,
        ocean_sea_anomaly,
        flux_sea_response,
        gll_tables(),
        jnp.asarray(order),
    )
    return (
        stepped.reshape(atmosphere_state.shape),
        layout.T,
        updated,
        atmos.reshape(COLS),
    )


def solution(mesh):
    placed = (
        P(None, None, ("sect", "dev")),
        P(None, ("sect", "dev")),
        P(),
        P(),
        P(),
        P(),
        P(),
        P(),
        P(("sect", "dev"), None),
        P(("sect", "dev"), None),
        P(),
    )
    return jax.shard_map(
        per_device,
        mesh=mesh,
        in_specs=placed,
        out_specs=(
            P(None, None, ("sect", "dev")),
            P(("sect", "dev"), None),
            P(("sect", "dev"), None),
            P(("sect", "dev")),
        ),
        check_vma=False,
    )
```

time: 558 us -> 53.5 us (0.10)
  blocking collectives: 352 us -> 0 us
  waiting for transfers between devices: 105 us -> 0 us
  local copies, waits for them, and re-layouts: 57 us -> 13.9 us
  Pallas kernels: 0 us -> 38.4 us
  between operations: 14.5 us -> 0.67 us
  matrix products: 11.2 us -> 0 us
  starting transfers between devices: 10.5 us -> 0 us
  other arithmetic: 7.34 us -> 0 us
    all_gather x1 -> x0, blocking collectives: 318 us -> none  [per_device(): lax.all_gather(ocean_cell_sea_temp, ('sect', 'dev'), axis=0, tiled=True)]
    all_gather x1 -> x0, waiting for transfers between devices: 76.3 us -> none  [per_device(): every_flux = lax.all_gather(col_flux, ('sect', 'dev'), axis=1, tiled=True)]
    pallas_call x0 -> x1, Pallas kernels: none -> 38.4 us  [per_device(): pl.pallas_call(kernel, out_shape=[jax.ShapeDtypeStruct((WIDTH, COLS), BF1...]
    all_to_all x1 -> x0, blocking collectives: 34.2 us -> none  [relay(): lax.all_to_all(outgoing, ('sect', 'dev'), split_axis=0, concat_axis=0, ti...]
    reshape x9 -> x0, local copies, waits for them, and re-layouts: 29.6 us -> none  [the longest x1 24.1 us: per_device(): picked = every_flux.reshape(nflux, total_blocks, BLOCK_CELLS)[:, source]]
    all_to_all x2 -> x0, waiting for transfers between devices: 28.3 us -> none  [the longest x1 18.6 us: per_device(): lax.all_to_all(updated, ('sect', 'dev'), split_axis=0, concat_axis=0, til...]
    dot_general x8 -> x0, matrix products: 11.2 us -> none  [the longest x1 4.14 us: physics(): jnp.dot(hidden, physics_tendency_layer, preferred_element_type=jnp.float32)]
    all_to_all x2 -> x0, starting transfers between devices: 10.5 us -> none  [the longest x1 6.17 us: per_device(): lax.all_to_all(fluxes, ('sect', 'dev'), split_axis=0, concat_axis=0, tile...]
  transfers between devices with their start and end apart: 3 -> 0, of which waited for: 3 -> 0; matrix products, arithmetic and copies ran while one was open for 3% -> 0% of each run, Pallas kernels for 0% -> 0%
where the time goes in v1:
time: 53.5 us; the launch traced here: 52.9 us
  Pallas kernels  38.4 us (72%)
  local copies, waits for them, and re-layouts  13.9 us (26%)
  between operations  0.67 us (1%)
    pallas_call x1, Pallas kernels, per_device(): pl.pallas_call(kernel, out_shape=[jax.ShapeDtypeStruct((WIDTH, COLS), BF1...  38.4 us
    unnamed x30, local copies, waits for them, and re-layouts  13.9 us

profile of v1, /device:TPU:1, one launch (start us, length us, event | category | flops | bytes accessed | tf_op | source)
XLA Modules:
  0.0 52.9 jit_solution(5707893952755558994)
XLA Ops:
  0.6 0.0 copy-start
  0.6 1.1 %copy-done = bf16[4,72,1024]{2,1,0:T(8,128)(2,1)S(1)} copy-done((bf16[4,72,1024]{2,1,0:T(8,128)(2,1)S(1)}, bf16[4,72,1024]{2,1,0:T(8,128)(2,1)}, u32[]{:S(2)}) %copy-start) | copy-done | bytes 589848
  1.7 0.0 copy-start.1
  1.7 1.1 %copy-done.1 = bf16[288,1024]{1,0:T(8,128)(2,1)S(1)} copy-done((bf16[288,1024]{1,0:T(8,128)(2,1)S(1)}, bf16[288,1024]{1,0:T(8,128)(2,1)}, u32[]{:S(2)}) %copy-start.1) | copy-done | bytes 589848
  2.8 0.0 copy-start.2
  2.8 1.1 %copy-done.2 = bf16[1024,288]{0,1:T(8,128)(2,1)S(1)} copy-done((bf16[1024,288]{0,1:T(8,128)(2,1)S(1)}, bf16[1024,288]{0,1:T(8,128)(2,1)}, u32[]{:S(2)}) %copy-start.2) | copy-done | bytes 589848
  3.8 0.0 copy-start.3
  3.8 1.0 %copy-done.3 = s32[131072,1]{0,1:T(1,128)S(1)} copy-done((s32[131072,1]{0,1:T(1,128)S(1)}, s32[131072,1]{0,1:T(1,128)}, u32[]{:S(2)}) %copy-start.3) | copy-done | bytes 524312
  4.9 0.0 copy-start.4
  4.9 0.8 %copy-done.4 = f32[128,128]{1,0:T(8,128)S(1)} copy-done((f32[128,128]{1,0:T(8,128)S(1)}, f32[128,128]{1,0:T(8,128)}, u32[]{:S(2)}) %copy-start.4) | copy-done | bytes 65560
  5.7 0.0 copy-start.5
  5.7 0.8 %copy-done.5 = bf16[128,256]{1,0:T(8,128)(2,1)S(1)} copy-done((bf16[128,256]{1,0:T(8,128)(2,1)S(1)}, bf16[128,256]{1,0:T(8,128)(2,1)}, u32[]{:S(2)}) %copy-start.5) | copy-done | bytes 65560
  6.6 0.0 copy-start.6
  6.6 0.8 %copy-done.6 = s32[128,8]{1,0:T(8,128)S(1)} copy-done((s32[128,8]{1,0:T(8,128)S(1)}, s32[128,8]{1,0:T(8,128)}, u32[]{:S(2)}) %copy-start.6) | copy-done | bytes 4120
  7.4 0.0 copy-start.7
  7.4 0.7 %copy-done.7 = f32[2,1024]{1,0:T(2,128)S(1)} copy-done((f32[2,1024]{1,0:T(2,128)S(1)}, f32[2,1024]{1,0:T(2,128)}, u32[]{:S(2)}) %copy-start.7) | copy-done | bytes 8216
  8.1 0.0 copy-start.8
  8.1 0.7 %copy-done.8 = bf16[1024,4]{0,1:T(4,128)(2,1)S(1)} copy-done((bf16[1024,4]{0,1:T(4,128)(2,1)S(1)}, bf16[1024,4]{0,1:T(4,128)(2,1)}, u32[]{:S(2)}) %copy-start.8) | copy-done | bytes 8216
  8.8 0.0 copy-start.9
  8.8 0.7 %copy-done.9 = s32[1024]{0:T(1024)S(1)} copy-done((s32[1024]{0:T(1024)S(1)}, s32[1024]{0:T(1024)}, u32[]{:S(2)}) %copy-start.9) | copy-done | bytes 4120
  9.5 0.0 copy-start.10
  9.5 0.7 %copy-done.10 = s32[8,128]{1,0:T(8,128)S(1)} copy-done((s32[8,128]{1,0:T(8,128)S(1)}, s32[8,128]{1,0:T(8,128)}, u32[]{:S(2)}) %copy-start.10) | copy-done | bytes 4120
  10.2 0.0 copy-start.11
  10.2 0.7 %copy-done.11 = f32[8,128]{1,0:T(8,128)S(1)} copy-done((f32[8,128]{1,0:T(8,128)S(1)}, f32[8,128]{1,0:T(8,128)}, u32[]{:S(2)}) %copy-start.11) | copy-done | bytes 4120
  10.8 0.0 copy-start.12
  10.9 0.7 %copy-done.12 = f32[4]{0:T(128)S(1)} copy-done((f32[4]{0:T(128)S(1)}, f32[4]{0:T(128)}, u32[]{:S(2)}) %copy-start.12) | copy-done | bytes 40
  11.5 38.4 %coupling_interval.1 = (bf16[288,1024]{1,0:T(8,128)(2,1)S(1)}, bf16[288,2048]{1,0:T(8,128)(2,1)S(1)}, f32[8,128]{1,0:T(8,128)S(1)}, f32[8,128]{1,0:T(8,128)S(1)}) custom-call(bf16[288,1024]{1,0:T(8,128)(2,1)S(1)} %bitcast.10, s32[128,8,128]{2,1,0:T(8,128)S(1)} %bitcast.12, bf16[288,1024]{1,0:T(8,128)(2,1)S(1)} %copy-done.1, bf16[288,1024]{1,0:T(8,128)(2,1)S(1)} %bitcast.11, ...), custom_call_target="tpu_custom_call" | custom-call | tf_op jit(solution)/shard_map/coupling_interval/pallas_call | solution.py:358
  49.9 0.8 %copy.21 = bf16[4,72,1024]{2,1,0:T(8,128)(2,1)} copy(bf16[4,72,1024]{2,1,0:T(8,128)(2,1)S(1)} %bitcast.9) | data formatting | bytes 1179648
  50.7 1.0 %copy.22 = bf16[2048,288]{0,1:T(8,128)(2,1)} copy(bf16[2048,288]{0,1:T(8,128)(2,1)S(1)} %bitcast.8) | data formatting | bytes 2359296
  51.7 0.6 %copy.23 = f32[8,128]{1,0:T(8,128)} copy(f32[8,128]{1,0:T(8,128)S(1)} %get-tuple-element.18) | data formatting | bytes 8192
  52.3 0.6 %copy.24 = f32[1024]{0:T(1024)} copy(f32[1024]{0:T(1024)S(1)} %bitcast.15) | data formatting | bytes 8192
Async XLA Ops:
  0.6 1.1 %copy-start = (bf16[4,72,1024]{2,1,0:T(8,128)(2,1)S(1)}, bf16[4,72,1024]{2,1,0:T(8,128)(2,1)}, u32[]{:S(2)}) copy-start(bf16[4,72,1024]{2,1,0:T(8,128)(2,1)} %param.13) | copy-start | bytes 1769476
  1.7 1.1 %copy-start.1 = (bf16[288,1024]{1,0:T(8,128)(2,1)S(1)}, bf16[288,1024]{1,0:T(8,128)(2,1)}, u32[]{:S(2)}) copy-start(bf16[288,1024]{1,0:T(8,128)(2,1)} %w1_hbm.1) | copy-start | bytes 1769476
  2.8 1.1 %copy-start.2 = (bf16[1024,288]{0,1:T(8,128)(2,1)S(1)}, bf16[1024,288]{0,1:T(8,128)(2,1)}, u32[]{:S(2)}) copy-start(bf16[1024,288]{0,1:T(8,128)(2,1)} %param.17) | copy-start | bytes 1769476
  3.8 1.0 %copy-start.3 = (s32[131072,1]{0,1:T(1,128)S(1)}, s32[131072,1]{0,1:T(1,128)}, u32[]{:S(2)}) copy-start(s32[131072,1]{0,1:T(1,128)} %param.15) | copy-start | bytes 1572868
  4.9 0.8 %copy-start.4 = (f32[128,128]{1,0:T(8,128)S(1)}, f32[128,128]{1,0:T(8,128)}, u32[]{:S(2)}) copy-start(f32[128,128]{1,0:T(8,128)} %remap_ref.1) | copy-start | bytes 196612
  5.7 0.8 %copy-start.5 = (bf16[128,256]{1,0:T(8,128)(2,1)S(1)}, bf16[128,256]{1,0:T(8,128)(2,1)}, u32[]{:S(2)}) copy-start(bf16[128,256]{1,0:T(8,128)(2,1)} %constant.8.deriv_ref) | copy-start | bytes 196612
  6.6 0.8 %copy-start.6 = (s32[128,8]{1,0:T(8,128)S(1)}, s32[128,8]{1,0:T(8,128)}, u32[]{:S(2)}) copy-start(s32[128,8]{1,0:T(8,128)} %constant.5.clone.order_ref) | copy-start | bytes 12292
  7.4 0.7 %copy-start.7 = (f32[2,1024]{1,0:T(2,128)S(1)}, f32[2,1024]{1,0:T(2,128)}, u32[]{:S(2)}) copy-start(f32[2,1024]{1,0:T(2,128)} %metric_ref.1) | copy-start | bytes 24580
  8.1 0.7 %copy-start.8 = (bf16[1024,4]{0,1:T(4,128)(2,1)S(1)}, bf16[1024,4]{0,1:T(4,128)(2,1)}, u32[]{:S(2)}) copy-start(bf16[1024,4]{0,1:T(4,128)(2,1)} %param.18) | copy-start | bytes 24580
  8.8 0.7 %copy-start.9 = (s32[1024]{0:T(1024)S(1)}, s32[1024]{0:T(1024)}, u32[]{:S(2)}) copy-start(s32[1024]{0:T(1024)} %param.19) | copy-start | bytes 12292
  9.5 0.7 %copy-start.10 = (s32[8,128]{1,0:T(8,128)S(1)}, s32[8,128]{1,0:T(8,128)}, u32[]{:S(2)}) copy-start(s32[8,128]{1,0:T(8,128)} %mask_ref.1) | copy-start | bytes 12292
  10.2 0.7 %copy-start.11 = (f32[8,128]{1,0:T(8,128)S(1)}, f32[8,128]{1,0:T(8,128)}, u32[]{:S(2)}) copy-start(f32[8,128]{1,0:T(8,128)} %anomaly_ref.1) | copy-start | bytes 12292
  10.8 0.7 %copy-start.12 = (f32[4]{0:T(128)S(1)}, f32[4]{0:T(128)}, u32[]{:S(2)}) copy-start(f32[4]{0:T(128)} %response_ref.1) | copy-start | bytes 52

commit v2 on v1

v2 whole, which is shorter than its diff:
```python
import functools
import itertools
import random

import jax
import jax.numpy as jnp
import numpy as np
from jax import lax
from jax.experimental import pallas as pl
from jax.experimental.pallas import tpu as pltpu
from jax.sharding import PartitionSpec as P

MESH = pl.DeviceIdType.MESH
BF16 = jnp.bfloat16
F32 = jnp.float32
I32 = jnp.int32

DEVICES = 128
CAP = 16
COLS = 1024
WIDTH = 288
HID = 1024
ROWS = 40
STEP = 256
VMEM_LIMIT = 32 * 1024 * 1024
NT = (((1,), (1,)), ((), ()))


def gll_tables():
    gll_nodes = np.array([-1.0, -1.0 / np.sqrt(5.0), 1.0 / np.sqrt(5.0), 1.0])
    offdiag = gll_nodes[:, None] - gll_nodes[None, :] + np.eye(4)
    bary = np.prod(offdiag, axis=1)
    derivative = bary[:, None] / (bary[None, :] * offdiag)
    diag_sum = np.sum(1.0 / offdiag - np.eye(4), axis=1)
    derivative = derivative * (1.0 - np.eye(4)) + np.eye(4) * diag_sum[:, None]
    first_dir = np.kron(np.eye(8), np.kron(np.eye(4), derivative)).T
    second_dir = np.kron(np.eye(8), np.kron(derivative, np.eye(4))).T
    return np.concatenate([first_dir, second_dir], axis=1)


QUARTERS = [[(0, 1), (0, 3)], [(1, 1), (1, 3)], [(0, 2), (0, 0)], [(1, 2), (1, 0)]]


def message_order():
    hops = lambda k: min(k, 4 - k)
    mixed, order = random.Random(1), []
    for planes in QUARTERS:
        part = [plane + yz for plane in planes for yz in itertools.product(range(4), range(4))]
        mixed.shuffle(part)
        part.sort(key=lambda o: (o == SELF, -sum(hops(k) for k in o[1:])))
        order += part
    return order


SELF = (0, 0, 0, 0)
ORDER = message_order()
FAR_FIRST = sorted(ORDER, key=lambda o: -sum(min(k, 4 - k) for k in o[1:]))
CHUNKS = [8, 24, 32, 32, 32]


def tables():
    table = np.zeros((DEVICES, 384), np.float32)
    table[:, :256] = gll_tables()
    table[:, 256:260] = ORDER
    return table


def device(index):
    return (lax.div(index, 64), lax.rem(index, 64))


def dot(a, b):
    return jnp.dot(a, b, preferred_element_type=F32)


def dot_nt(a, b, precision=None):
    return lax.dot_general(a, b, NT, precision=precision, preferred_element_type=F32)


def iota(shape, dim):
    return lax.broadcasted_iota(I32, shape, dim)


def one_hot(condition):
    return jnp.where(condition, 1.0, 0.0).astype(BF16)


def kernel(
    target_hbm,
    table_hbm,
    w1_hbm,
    state_hbm,
    metric_hbm,
    w2t_hbm,
    w3t_hbm,
    response_hbm,
    tile_hbm,
    mask_hbm,
    anomaly_hbm,
    remap_hbm,
    stepped_out,
    layout_out,
    updated_out,
    atmos_out,
    target_v,
    table_v,
    w1_v,
    x_v,
    metric_v,
    w23_v,
    w3t_v,
    response_v,
    tile_v,
    mask_v,
    anomaly_v,
    remap_v,
    w1t_v,
    adv_v,
    hid_v,
    tend_v,
    step_v,
    lay_v,
    q_v,
    updated_v,
    atmos_v,
    send_v,
    recv_v,
    near_send,
    near_recv,
    far_send,
    far_recv,
    in_sem,
    out_sem,
    lay_sem,
    send_sem,
    recv_sem,
    near_sem,
    far_sem,
):
    core, chip = lax.axis_index("sect"), lax.axis_index("dev")
    me = core * 64 + chip
    high, low = lax.div(me, 8), lax.rem(me, 8)
    x, y, z = lax.div(chip, 16), lax.rem(lax.div(chip, 4), 4), lax.rem(chip, 4)

    pairs = [
        (target_hbm.at[me], target_v),
        (table_hbm, table_v),
        (w1_hbm, w1_v),
        (state_hbm, x_v),
        (metric_hbm, metric_v),
        (w2t_hbm, w23_v.at[pl.ds(0, WIDTH)]),
        (w3t_hbm, w3t_v),
        (response_hbm, response_v),
        (tile_hbm, tile_v),
        (mask_hbm, mask_v),
        (anomaly_hbm, anomaly_v),
        (remap_hbm, remap_v),
    ]
    loads = [pltpu.make_async_copy(a, b, in_sem.at[i]) for i, (a, b) in enumerate(pairs)]
    for load in loads:
        load.start()

    cores = [lax.rem(core + k, 2) for k in range(2)]
    xs = [lax.rem(x + k, 4) * 16 for k in range(4)]
    ys = [lax.rem(y + k, 4) * 4 for k in range(4)]
    zs = [lax.rem(z + k, 4) for k in range(4)]
    barrier = pltpu.get_barrier_semaphore()
    for a, b, e, f in FAR_FIRST:
        if (a, b, e, f) != SELF:
            pl.semaphore_signal(barrier, inc=1, device_id=(cores[a], xs[b] + ys[e] + zs[f]), device_id_type=MESH)

    loads[0].wait()
    loads[1].wait()
    order = table_v[:, 256:384].astype(I32)
    to_device = (
        ((order[:, 0:1] + core) & 1) * 64
        + ((order[:, 1:2] + x) & 3) * 16
        + ((order[:, 2:3] + y) & 3) * 4
        + ((order[:, 3:4] + z) & 3)
    )

    targets = jnp.concatenate([target_v[k : k + 1, :] for k in range(8)], axis=1)
    before = one_hot(iota((STEP, STEP), 0) < iota((STEP, STEP), 1))
    message = iota((DEVICES, STEP), 0)
    taken = jnp.zeros((DEVICES, 1), F32)
    slots = []
    for c in range(COLS // STEP):
        hit = to_device == targets[:, c * STEP : (c + 1) * STEP]
        hits = jnp.where(hit, 1.0, 0.0)
        earlier = dot(hits.astype(BF16), before) + taken
        taken = taken + jnp.sum(hits, axis=1, keepdims=True)
        slot = jnp.where(hit, earlier.astype(I32) + CAP * message, 0)
        slots.append(jnp.sum(slot, axis=0, keepdims=True))
    slots = jnp.concatenate(slots, axis=1)

    loads[2].wait()
    unit = one_hot(iota((256, 256), 0) == iota((256, 256), 1))
    for b in range(HID // 256):
        rows = slice(b * 256, (b + 1) * 256)
        w1t_v[rows, :] = dot_nt(unit, w1_v[:, rows]).astype(BF16)

    for load in loads[3:8]:
        load.wait()
    w3t = w3t_v[...].astype(F32)
    w23_v[WIDTH : WIDTH + 16, :] = jnp.concatenate([w3t, jnp.zeros((12, HID), F32)], axis=0).astype(BF16)
    deriv = table_v[:, 0:256].astype(BF16)
    stores = []
    for c in range(COLS // STEP):
        for b in range(STEP // 128):
            at = slice(c * STEP + b * 128, c * STEP + (b + 1) * 128)
            field = x_v[:, at]
            grads = dot(field, deriv)
            wide = field.astype(F32)
            wind_first = wide[0:72] * metric_v[0:1, at]
            wind_second = wide[72:144] * metric_v[1:2, at]
            moved = (
                wide
                - jnp.concatenate([wind_first] * 4, axis=0) * grads[:, 0:128]
                - jnp.concatenate([wind_second] * 4, axis=0) * grads[:, 128:256]
            )
            adv_v[:, at] = moved.astype(BF16)
        at = slice(c * STEP, (c + 1) * STEP)
        column = adv_v[:, at]
        for b in range(HID // 256):
            rows = slice(b * 256, (b + 1) * 256)
            half = 0.5 * dot(w1t_v[rows, :], column)
            hid_v[rows, at] = (half + half * jnp.tanh(half)).astype(BF16)
        result = dot(w23_v[...], hid_v[:, at])
        tendency = result[0:WIDTH]
        step_v[:, at] = (column.astype(F32) + tendency).astype(BF16)
        tendency = tendency.astype(BF16)
        tend_v[0:WIDTH, at] = tendency
        for g in range(1, 4):
            tend_v[256 + 32 * g : 288 + 32 * g, at] = tendency[256:288]
        flux = result[WIDTH : WIDTH + 8].astype(BF16).astype(F32)
        mixed = sum(response_v[:, k : k + 1] * flux[k : k + 1] for k in range(4))
        for b in range(STEP // 128):
            j = c * (STEP // 128) + b
            q_v[j : j + 1, :] = mixed[:, b * 128 : (b + 1) * 128]
        store = pltpu.make_async_copy(step_v.at[:, at], stepped_out.at[:, at], out_sem.at[c])
        store.start()
        stores.append(store)

    for load in loads[8:]:
        load.wait()
    lane, sub = iota((8, 128), 1), iota((8, 128), 0)
    shift_row = jnp.where(iota((1, 128), 1) < 8, tile_v[0:1, :] >> 3, -1)
    shift_col = jnp.sum(jnp.where(lane == sub, shift_row, 0), axis=1, keepdims=True)
    same = jnp.where((shift_row == shift_col) & (lane < 8), 1, 0)
    twin_row = jnp.sum(jnp.where(sub < lane, same, 0), axis=0, keepdims=True)
    twin_col = jnp.sum(jnp.where(lane < sub, same, 0), axis=1, keepdims=True)

    ocean = mask_v[...].astype(F32)
    ahead = jnp.concatenate([ocean, ocean * anomaly_v[...]], axis=0).astype(BF16)
    near_send[...] = ahead
    near_recv[low] = ahead

    q = q_v[...]
    q_rows = jnp.concatenate([q, jnp.zeros((120, 128), F32)], axis=0).astype(BF16)
    flux_to = jnp.where(shift_row < 0, -1, (shift_row + me) & (DEVICES - 1))
    flux_rows = [dot(one_hot((to_device == flux_to) & (twin_row == u)), q_rows) for u in range(2)]

    pl.semaphore_wait(barrier, DEVICES - 1)

    for i in range(1, 8):
        pltpu.make_async_remote_copy(
            near_send,
            near_recv.at[low],
            near_sem.at[0],
            near_sem.at[1],
            device_id=device(high * 8 + lax.rem(low + i, 8)),
            device_id_type=MESH,
        ).start()

    plane = lax.div(me, 16)
    first = 0
    for k, count in enumerate(CHUNKS):
        size = count * CAP
        pick = one_hot(iota((size, COLS), 0) + first * CAP == slots)
        placed = dot_nt(pick, tend_v[...])
        into = pl.ds(first, count)
        main = placed[:, 0:256].astype(BF16)
        send_v[into, 0:16, :] = main[:, 0:128].reshape(count, CAP, 128)
        send_v[into, 16:32, :] = main[:, 128:256].reshape(count, CAP, 128)
        keep = (iota((size, 128), 0) & 15) >> 2 == iota((size, 128), 1) >> 5
        tail = jnp.where(keep, placed[:, 256:384], 0.0).reshape(count, CAP, 128)
        tail = tail[:, 0:8] + tail[:, 8:16]
        tail = tail + jnp.concatenate([tail[:, 4:8], tail[:, 0:4]], axis=1)
        packed_row = iota((count, 8, 128), 1)
        for u in range(2):
            row = flux_rows[u][first : first + count].reshape(count, 1, 128)
            tail = jnp.where(packed_row == 4 + u, row, tail)
        send_v[into, 32:40, :] = tail.astype(BF16)
        for i in range(first, first + count):
            a, b, e, f = ORDER[i]
            if ORDER[i] == SELF:
                pltpu.make_async_copy(send_v.at[i], recv_v.at[me], recv_sem.at[plane]).start()
                continue
            pltpu.make_async_remote_copy(
                send_v.at[i],
                recv_v.at[me],
                send_sem,
                recv_sem.at[plane],
                device_id=(cores[a], xs[b] + ys[e] + zs[f]),
                device_id_type=MESH,
            ).start()
        first += count
        if k == 2:
            got = near_recv.at[pl.ds(0, 7)]
            pltpu.make_async_copy(got, got, near_sem.at[1]).wait()
            source = (low + shift_col) & 7
            source = jnp.concatenate([source, source], axis=0)
            chosen = jnp.zeros((16, 128), F32)
            for l in range(8):
                chosen = chosen + jnp.where(source == l, near_recv[l].astype(F32), 0.0)
            chosen = chosen.astype(BF16)
            far_send[...] = chosen
            far_recv[high] = chosen
            for i in range(1, 16):
                pltpu.make_async_remote_copy(
                    far_send,
                    far_recv.at[high],
                    far_sem.at[0],
                    far_sem.at[1],
                    device_id=device(lax.rem(high + i, 16) * 8 + low),
                    device_id_type=MESH,
                ).start()

    slot, row = iota((256, 128), 0), iota((256, 128), 1)
    spread = one_hot((row >> 3 == slot >> 4) & ((row & 7) == (slot & 3)))
    held = (slot & 15) >> 2 == row >> 5
    fold = one_hot(iota((32, 128), 0) == (iota((32, 128), 1) & 31))
    flux_row = ((me - shift_col) & (DEVICES - 1)) * 8 + 4 + twin_col
    remap = remap_v[...]
    received = jnp.zeros((8, 128), F32)
    for quarter, planes in enumerate(QUARTERS):
        for a, b in planes:
            group = cores[a] * 4 + lax.rem(x - b + 4, 4)
            sixteen = pl.ds(pl.multiple_of(group * 16, 16), 16)
            got = recv_v.at[sixteen]
            pltpu.make_async_copy(got, got, recv_sem.at[group]).wait()
            lanes = pl.ds(pl.multiple_of(group * 256, 256), 256)
            main = jnp.concatenate(
                [recv_v[sixteen, 16 * h : 16 * h + 16, :].reshape(256, 128) for h in range(2)], axis=1
            )
            lay_v[0:256, lanes] = dot_nt(unit, main).astype(BF16)
            packed = recv_v[sixteen, 32:40, :].astype(F32).reshape(128, 128).astype(BF16)
            wide = jnp.where(held, dot(spread, packed), 0.0).astype(BF16)
            lay_v[256:288, lanes] = dot_nt(fold, wide).astype(BF16)
            received = received + dot(one_hot(iota((8, 128), 1) + group * 128 == flux_row), packed)
            pltpu.make_async_copy(lay_v.at[:, lanes], layout_out.at[:, lanes], lay_sem).start()
        if quarter == 2:
            got = far_recv.at[pl.ds(0, 15)]
            pltpu.make_async_copy(got, got, far_sem.at[1]).wait()
            source = ((me + shift_col) & (DEVICES - 1)) >> 3
            source = jnp.concatenate([source, source], axis=0)
            chosen = jnp.zeros((16, 128), F32)
            for h in range(16):
                chosen = chosen + jnp.where(source == h, far_recv[h].astype(F32), 0.0)
            cell = dot_nt(q, remap, lax.Precision.HIGHEST)
            masked = chosen[8:16] + chosen[0:8] * cell
            atmos_v[...] = jnp.dot(masked, remap, precision=lax.Precision.HIGHEST, preferred_element_type=F32)
            stores.append(pltpu.make_async_copy(atmos_v, atmos_out, out_sem.at[4]))
            stores[-1].start()

    cell = dot_nt(received, remap, lax.Precision.HIGHEST)
    updated_v[...] = anomaly_v[...] + mask_v[...].astype(F32) * cell
    stores.append(pltpu.make_async_copy(updated_v, updated_out, out_sem.at[5]))
    stores[-1].start()

    sent = send_v.at[pl.ds(0, DEVICES - 1)]
    pltpu.make_async_copy(sent, sent, send_sem).wait()
    sent = near_recv.at[pl.ds(0, 7)]
    pltpu.make_async_copy(sent, sent, near_sem.at[0]).wait()
    sent = far_recv.at[pl.ds(0, 15)]
    pltpu.make_async_copy(sent, sent, far_sem.at[0]).wait()
    for store in stores:
        store.wait()
    pltpu.make_async_copy(lay_v, layout_out, lay_sem).wait()


def hand_out(a, b, c, d, a_out, b_out, c_out, d_out, sem):
    copies = [
        pltpu.make_async_copy(source, result, sem.at[i])
        for i, (source, result) in enumerate(((b, b_out), (a, a_out), (c, c_out), (d, d_out)))
    ]
    for copy in copies:
        copy.start()
    for copy in copies:
        copy.wait()


def per_device(
    atmosphere_state,
    metric,
    column_group_target,
    physics_input_layer,
    physics_tendency_layer,
    physics_flux_layer,
    block_to_tile,
    remap_weight_matrix,
    ocean_land_mask,
    ocean_sea_anomaly,
    flux_sea_response,
):
    anywhere, hbm = pl.BlockSpec(memory_space=pl.ANY), pl.BlockSpec(memory_space=pltpu.HBM)
    results = [
        jax.ShapeDtypeStruct((WIDTH, COLS), BF16),
        jax.ShapeDtypeStruct((WIDTH, DEVICES * CAP), BF16),
        jax.ShapeDtypeStruct((8, 128), F32),
        jax.ShapeDtypeStruct((8, 128), F32),
    ]
    done = pl.pallas_call(
        kernel,
        out_shape=results,
        in_specs=[hbm] * 12,
        out_specs=[anywhere] * 4,
        scratch_shapes=[
            pltpu.VMEM((8, 128), I32),
            pltpu.VMEM((DEVICES, 384), F32),
            pltpu.VMEM((WIDTH, HID), BF16),
            pltpu.VMEM((WIDTH, COLS), BF16),
            pltpu.VMEM((2, COLS), F32),
            pltpu.VMEM((WIDTH + 16, HID), BF16),
            pltpu.VMEM((4, HID), BF16),
            pltpu.VMEM((1, 4), F32),
            pltpu.VMEM((8, 128), I32),
            pltpu.VMEM((8, 128), I32),
            pltpu.VMEM((8, 128), F32),
            pltpu.VMEM((128, 128), F32),
            pltpu.VMEM((HID, WIDTH), BF16),
            pltpu.VMEM((WIDTH, COLS), BF16),
            pltpu.VMEM((HID, COLS), BF16),
            pltpu.VMEM((384, COLS), BF16),
            pltpu.VMEM((WIDTH, COLS), BF16),
            pltpu.VMEM((WIDTH, DEVICES * CAP), BF16),
            pltpu.VMEM((8, 128), F32),
            pltpu.VMEM((8, 128), F32),
            pltpu.VMEM((8, 128), F32),
            pltpu.VMEM((DEVICES, ROWS, 128), BF16),
            pltpu.VMEM((DEVICES, ROWS, 128), BF16),
            pltpu.VMEM((16, 128), BF16),
            pltpu.VMEM((8, 16, 128), BF16),
            pltpu.VMEM((16, 128), BF16),
            pltpu.VMEM((16, 16, 128), BF16),
            pltpu.SemaphoreType.DMA((12,)),
            pltpu.SemaphoreType.DMA((6,)),
            pltpu.SemaphoreType.DMA,
            pltpu.SemaphoreType.DMA,
            pltpu.SemaphoreType.DMA((8,)),
            pltpu.SemaphoreType.DMA((2,)),
            pltpu.SemaphoreType.DMA((2,)),
        ],
        compiler_params=pltpu.CompilerParams(
            collective_id=0, has_side_effects=True, vmem_limit_bytes=VMEM_LIMIT
        ),
        name="coupling_interval",
    )(*[pltpu.with_memory_space_constraint(v, pltpu.HBM) for v in (
        column_group_target.reshape(DEVICES, 8, 128),
        jnp.asarray(tables()),
        physics_input_layer,
        atmosphere_state.reshape(WIDTH, COLS),
        metric,
        physics_tendency_layer.T,
        physics_flux_layer.T,
        flux_sea_response.reshape(1, 4),
        block_to_tile.reshape(8, 128),
        ocean_land_mask,
        ocean_sea_anomaly,
        remap_weight_matrix,
    )])
    stepped, layout, updated, atmos = pl.pallas_call(
        hand_out,
        out_shape=results,
        in_specs=[anywhere] * 4,
        out_specs=[anywhere] * 4,
        scratch_shapes=[pltpu.SemaphoreType.DMA((4,))],
        compiler_params=pltpu.CompilerParams(vmem_limit_bytes=4 * 1024 * 1024),
        name="hand_out",
    )(*done)
    return (
        stepped.reshape(atmosphere_state.shape),
        layout.T,
        updated,
        atmos.reshape(COLS),
    )


def solution(mesh):
    placed = (
        P(None, None, ("sect", "dev")),
        P(None, ("sect", "dev")),
        P(),
        P(),
        P(),
        P(),
        P(),
        P(),
        P(("sect", "dev"), None),
        P(("sect", "dev"), None),
        P(),
    )
    return jax.shard_map(
        per_device,
        mesh=mesh,
        in_specs=placed,
        out_specs=(
            P(None, None, ("sect", "dev")),
            P(("sect", "dev"), None),
            P(("sect", "dev"), None),
            P(("sect", "dev")),
        ),
        check_vma=False,
    )
```

time: 53.5 us -> 35.3 us (0.66)
  local copies, waits for them, and re-layouts: 13.9 us -> 0 us
  Pallas kernels: 38.4 us -> 34.5 us
    unnamed x30 -> x0, local copies, waits for them, and re-layouts: 13.9 us -> none
    pallas_call x1 -> x2, Pallas kernels: 38.4 us -> 34.5 us  [the longest x1 33.3 us: per_device(): pl.pallas_call(kernel, out_shape=results, in_specs=[hbm] * 12, out_specs=...]
where the time goes in v2:
time: 35.3 us; the launch traced here: 35.2 us
  Pallas kernels  34.5 us (98%)
  between operations  0.64 us (2%)
    pallas_call x1, Pallas kernels, per_device(): pl.pallas_call(kernel, out_shape=results, in_specs=[hbm] * 12, out_specs=...  33.3 us
    pallas_call x1, Pallas kernels, per_device(): pl.pallas_call(hand_out, out_shape=results, in_specs=[anywhere] * 4, out_...  1.24 us

profile of v2, /device:TPU:1, one launch (start us, length us, event | category | flops | bytes accessed | tf_op | source)
XLA Modules:
  0.0 35.2 jit_solution(13519799865161194368)
XLA Ops:
  0.6 33.3 %coupling_interval.1 = (bf16[288,1024]{1,0:T(8,128)(2,1)S(1)}, bf16[288,2048]{1,0:T(8,128)(2,1)S(1)}, f32[8,128]{1,0:T(8,128)S(1)}, f32[8,128]{1,0:T(8,128)S(1)}) custom-call(s32[128,8,128]{2,1,0:T(8,128)} %bitcast.11, f32[128,384]{1,0:T(8,128)} %constant.2.clone.table_hbm, bf16[288,1024]{1,0:T(8,128)(2,1)} %w1_hbm.1, bf16[288,1024]{1,0:T(8,128)(2,1)} %bitcast.9, ...), custom_call_target="tpu_custom_call" | custom-call | tf_op jit(solution)/shard_map/coupling_interval/pallas_call | solution.py:413
  33.9 1.2 %hand_out.1 = (bf16[288,1024]{1,0:T(8,128)(2,1)}, bf16[288,2048]{1,0:T(8,128)(2,1)}, f32[8,128]{1,0:T(8,128)}, f32[8,128]{1,0:T(8,128)}) custom-call(bf16[288,1024]{1,0:T(8,128)(2,1)S(1)} %get-tuple-element.12.a, bf16[288,2048]{1,0:T(8,128)(2,1)S(1)} %get-tuple-element.13.b, f32[8,128]{1,0:T(8,128)S(1)} %get-tuple-element.14.c, f32[8,128]{1,0:T(8,128)S(1)} %get-tuple-element.15.d), custom_call_target="tpu_custom_call" | custom-call | tf_op jit(solution)/shard_map/hand_out/pallas_call | solution.py:472

commit v3 on v2

v3 whole, which is shorter than its diff:
```python
import functools
import itertools
import random

import jax
import jax.numpy as jnp
import numpy as np
from jax import lax
from jax.experimental import pallas as pl
from jax.experimental.pallas import tpu as pltpu
from jax.sharding import PartitionSpec as P

MESH = pl.DeviceIdType.MESH
BF16 = jnp.bfloat16
F32 = jnp.float32
I32 = jnp.int32

DEVICES = 128
CAP = 16
COLS = 1024
WIDTH = 288
HID = 1024
ROWS = 40
STEP = 256
WIDE = 512
VMEM_LIMIT = 32 * 1024 * 1024
NT = (((1,), (1,)), ((), ()))


def gll_tables():
    gll_nodes = np.array([-1.0, -1.0 / np.sqrt(5.0), 1.0 / np.sqrt(5.0), 1.0])
    offdiag = gll_nodes[:, None] - gll_nodes[None, :] + np.eye(4)
    bary = np.prod(offdiag, axis=1)
    derivative = bary[:, None] / (bary[None, :] * offdiag)
    diag_sum = np.sum(1.0 / offdiag - np.eye(4), axis=1)
    derivative = derivative * (1.0 - np.eye(4)) + np.eye(4) * diag_sum[:, None]
    first_dir = np.kron(np.eye(8), np.kron(np.eye(4), derivative)).T
    second_dir = np.kron(np.eye(8), np.kron(derivative, np.eye(4))).T
    return np.concatenate([first_dir, second_dir], axis=1)


QUARTERS = [[(0, 1), (0, 3)], [(1, 1), (1, 3)], [(0, 2), (0, 0)], [(1, 2), (1, 0)]]


def message_order():
    hops = lambda k: min(k, 4 - k)
    mixed, order = random.Random(1), []
    for planes in QUARTERS:
        part = [plane + yz for plane in planes for yz in itertools.product(range(4), range(4))]
        mixed.shuffle(part)
        part.sort(key=lambda o: (o == SELF, -sum(hops(k) for k in o[1:])))
        order += part
    return order


SELF = (0, 0, 0, 0)
ORDER = message_order()
FAR_FIRST = sorted(ORDER, key=lambda o: -sum(min(k, 4 - k) for k in o[1:]))
CHUNKS = [8, 24, 32, 32, 32]


def tables():
    table = np.zeros((DEVICES, 384), np.float32)
    table[:, :256] = gll_tables()
    table[:, 256:260] = ORDER
    return table


def device(index):
    return (lax.div(index, 64), lax.rem(index, 64))


def dot(a, b):
    return jnp.dot(a, b, preferred_element_type=F32)


def dot_nt(a, b, precision=None):
    return lax.dot_general(a, b, NT, precision=precision, preferred_element_type=F32)


def iota(shape, dim):
    return lax.broadcasted_iota(I32, shape, dim)


def one_hot(condition):
    return jnp.where(condition, 1.0, 0.0).astype(BF16)


def kernel(
    target_hbm,
    table_hbm,
    w1_hbm,
    state_hbm,
    metric_hbm,
    w2t_hbm,
    w3t_hbm,
    response_hbm,
    tile_hbm,
    mask_hbm,
    anomaly_hbm,
    remap_hbm,
    stepped_out,
    layout_out,
    updated_out,
    atmos_out,
    target_v,
    table_v,
    w1_v,
    x_v,
    metric_v,
    w23_v,
    w3t_v,
    response_v,
    tile_v,
    mask_v,
    anomaly_v,
    remap_v,
    w1t_v,
    adv_v,
    hid_v,
    tend_v,
    q_v,
    send_v,
    recv_v,
    ahead_send,
    ahead_recv,
    in_sem,
    send_sem,
    recv_sem,
    ahead_sent,
    ahead_sem,
):
    core, chip = lax.axis_index("sect"), lax.axis_index("dev")
    me = core * 64 + chip
    x, y, z = lax.div(chip, 16), lax.rem(lax.div(chip, 4), 4), lax.rem(chip, 4)

    half = COLS // 2
    pairs = [
        (state_hbm.at[:, pl.ds(0, half)], x_v.at[:, pl.ds(0, half)]),
        (state_hbm.at[:, pl.ds(half, half)], x_v.at[:, pl.ds(half, half)]),
        (metric_hbm, metric_v),
        (table_hbm, table_v),
        (w1_hbm.at[:, pl.ds(0, half)], w1_v.at[:, pl.ds(0, half)]),
        (w1_hbm.at[:, pl.ds(half, half)], w1_v.at[:, pl.ds(half, half)]),
        (target_hbm.at[me], target_v),
        (w2t_hbm.at[:, pl.ds(0, half)], w23_v.at[pl.ds(0, WIDTH), pl.ds(0, half)]),
        (w2t_hbm.at[:, pl.ds(half, half)], w23_v.at[pl.ds(0, WIDTH), pl.ds(half, half)]),
        (w3t_hbm, w3t_v),
        (response_hbm, response_v),
        (tile_hbm, tile_v),
        (mask_hbm, mask_v),
        (anomaly_hbm, anomaly_v),
        (remap_hbm, remap_v),
    ]
    loads = [pltpu.make_async_copy(a, b, in_sem.at[i]) for i, (a, b) in enumerate(pairs)]
    for load in loads:
        load.start()

    cores = [lax.rem(core + k, 2) for k in range(2)]
    xs = [lax.rem(x + k, 4) * 16 for k in range(4)]
    ys = [lax.rem(y + k, 4) * 4 for k in range(4)]
    zs = [lax.rem(z + k, 4) for k in range(4)]
    barrier = pltpu.get_barrier_semaphore()
    for a, b, e, f in FAR_FIRST:
        if (a, b, e, f) != SELF:
            pl.semaphore_signal(barrier, inc=1, device_id=(cores[a], xs[b] + ys[e] + zs[f]), device_id_type=MESH)

    for load in loads[0:4]:
        load.wait()
    deriv = table_v[:, 0:256].astype(BF16)

    def dynamics(b):
        at = slice(b * 128, (b + 1) * 128)
        field = x_v[:, at]
        grads = dot(field, deriv)
        wide = field.astype(F32)
        wind_first = wide[0:72] * metric_v[0:1, at]
        wind_second = wide[72:144] * metric_v[1:2, at]
        moved = (
            wide
            - jnp.concatenate([wind_first] * 4, axis=0) * grads[:, 0:128]
            - jnp.concatenate([wind_second] * 4, axis=0) * grads[:, 128:256]
        )
        adv_v[:, at] = moved.astype(BF16)

    def first_layer(c, b):
        at, rows = slice(c * WIDE, (c + 1) * WIDE), slice(b * 256, (b + 1) * 256)
        half = 0.5 * dot(w1t_v[rows, :], adv_v[:, at])
        hid_v[rows, at] = (half + half * jnp.tanh(half)).astype(BF16)

    def second_layer(c):
        at = slice(c * WIDE, (c + 1) * WIDE)
        result = dot(w23_v[...], hid_v[:, at])
        tendency = result[0:WIDTH]
        stepped_out[:, at] = (adv_v[:, at].astype(F32) + tendency).astype(BF16)
        tendency = tendency.astype(BF16)
        tend_v[0:WIDTH, at] = tendency
        for g in range(1, 4):
            tend_v[256 + 32 * g : 288 + 32 * g, at] = tendency[256:288]
        flux = result[WIDTH : WIDTH + 8].astype(BF16).astype(F32)
        mixed = sum(response_v[:, k : k + 1] * flux[k : k + 1] for k in range(4))
        for b in range(WIDE // 128):
            j = c * (WIDE // 128) + b
            q_v[j : j + 1, :] = mixed[:, b * 128 : (b + 1) * 128]

    for b in range(WIDE // 128):
        dynamics(b)

    for load in loads[4:7]:
        load.wait()
    unit = one_hot(iota((256, 256), 0) == iota((256, 256), 1))
    for b in range(HID // 256):
        rows = slice(b * 256, (b + 1) * 256)
        w1t_v[rows, :] = dot_nt(unit, w1_v[:, rows]).astype(BF16)

    for c in range(COLS // WIDE):
        for b in range(HID // 256):
            first_layer(c, b)
            if c + 1 < COLS // WIDE:
                for d in range(WIDE // 512):
                    dynamics((c + 1) * WIDE // 128 + b * (WIDE // 512) + d)
        if c == 0:
            for load in loads[7:]:
                load.wait()
            w3t = w3t_v[...].astype(F32)
            w23_v[WIDTH : WIDTH + 16, :] = jnp.concatenate([w3t, jnp.zeros((12, HID), F32)], axis=0).astype(BF16)
        else:
            second_layer(c - 1)
    order = table_v[:, 256:384].astype(I32)
    to_device = (
        ((order[:, 0:1] + core) & 1) * 64
        + ((order[:, 1:2] + x) & 3) * 16
        + ((order[:, 2:3] + y) & 3) * 4
        + ((order[:, 3:4] + z) & 3)
    )

    targets = jnp.concatenate([target_v[k : k + 1, :] for k in range(8)], axis=1)
    before = one_hot(iota((STEP, STEP), 0) < iota((STEP, STEP), 1))
    message = iota((DEVICES, STEP), 0)
    taken = jnp.zeros((DEVICES, 1), F32)
    slots = []
    for c in range(COLS // STEP):
        hit = to_device == targets[:, c * STEP : (c + 1) * STEP]
        hits = jnp.where(hit, 1.0, 0.0)
        earlier = dot(hits.astype(BF16), before) + taken
        taken = taken + jnp.sum(hits, axis=1, keepdims=True)
        slot = jnp.where(hit, earlier.astype(I32) + CAP * message, 0)
        slots.append(jnp.sum(slot, axis=0, keepdims=True))
    slots = jnp.concatenate(slots, axis=1)

    second_layer(COLS // WIDE - 1)

    lane, sub = iota((8, 128), 1), iota((8, 128), 0)
    shift_row = jnp.where(iota((1, 128), 1) < 8, tile_v[0:1, :] >> 3, -1)
    shift_col = jnp.sum(jnp.where(lane == sub, shift_row, 0), axis=1, keepdims=True)
    same = jnp.where((shift_row == shift_col) & (lane < 8), 1, 0)
    twin_row = jnp.sum(jnp.where(sub < lane, same, 0), axis=0, keepdims=True)
    twin_col = jnp.sum(jnp.where(lane < sub, same, 0), axis=1, keepdims=True)

    ocean = mask_v[...].astype(F32)
    ahead = jnp.concatenate([ocean, ocean * anomaly_v[...]], axis=0).astype(BF16)
    tile_device = (me + jnp.concatenate([shift_col, shift_col], axis=0)) & (DEVICES - 1)
    plane = lax.div(me, 16)
    steps = [
        (4, z, tile_device & 3, lambda k: plane * 16 + y * 4 + k),
        (4, y, (tile_device >> 2) & 3, lambda k: plane * 16 + k * 4 + z),
        (8, plane, tile_device >> 4, lambda k: k * 16 + y * 4 + z),
    ]

    def ocean_send(n, rows):
        size, mine, _, peer = steps[n]
        ahead_send[n] = rows
        ahead_recv[4 * n + mine] = rows
        for k in range(1, size):
            pltpu.make_async_remote_copy(
                ahead_send.at[n],
                ahead_recv.at[4 * n + mine],
                ahead_sent.at[n],
                ahead_sem.at[n],
                device_id=device(peer(lax.rem(mine + k, size))),
                device_id_type=MESH,
            ).start()

    def ocean_receive(n):
        size, _, source, _ = steps[n]
        got = ahead_recv.at[pl.ds(4 * n, size - 1)]
        pltpu.make_async_copy(got, got, ahead_sem.at[n]).wait()
        chosen = jnp.zeros((16, 128), F32)
        for k in range(size):
            chosen = chosen + jnp.where(source == k, ahead_recv[4 * n + k].astype(F32), 0.0)
        return chosen

    remap = remap_v[...]
    cell = dot_nt(q_v[...], remap, lax.Precision.HIGHEST)
    cell_rows = jnp.concatenate([cell, jnp.zeros((120, 128), F32)], axis=0).astype(BF16)
    cell_to = jnp.where(shift_row < 0, -1, (shift_row + me) & (DEVICES - 1))
    cell_rows = [dot(one_hot((to_device == cell_to) & (twin_row == u)), cell_rows) for u in range(2)]

    pl.semaphore_wait(barrier, DEVICES - 1)

    ocean_send(0, ahead)

    first = 0
    for k, count in enumerate(CHUNKS):
        size = count * CAP
        pick = one_hot(iota((size, COLS), 0) + first * CAP == slots)
        placed = dot_nt(pick, tend_v[...])
        into = pl.ds(first, count)
        main = placed[:, 0:256].astype(BF16)
        send_v[into, 0:16, :] = main[:, 0:128].reshape(count, CAP, 128)
        send_v[into, 16:32, :] = main[:, 128:256].reshape(count, CAP, 128)
        keep = (iota((size, 128), 0) & 15) >> 2 == iota((size, 128), 1) >> 5
        tail = jnp.where(keep, placed[:, 256:384], 0.0).reshape(count, CAP, 128)
        tail = tail[:, 0:8] + tail[:, 8:16]
        tail = tail + jnp.concatenate([tail[:, 4:8], tail[:, 0:4]], axis=1)
        packed_row = iota((count, 8, 128), 1)
        for u in range(2):
            row = cell_rows[u][first : first + count].reshape(count, 1, 128)
            tail = jnp.where(packed_row == 4 + u, row, tail)
        send_v[into, 32:40, :] = tail.astype(BF16)
        for i in range(first, first + count):
            a, b, e, f = ORDER[i]
            if ORDER[i] == SELF:
                pltpu.make_async_copy(send_v.at[i], recv_v.at[me], recv_sem.at[plane]).start()
                continue
            pltpu.make_async_remote_copy(
                send_v.at[i],
                recv_v.at[me],
                send_sem,
                recv_sem.at[plane],
                device_id=(cores[a], xs[b] + ys[e] + zs[f]),
                device_id_type=MESH,
            ).start()
        first += count
        if k in (2, 3):
            ocean_send(k - 1, ocean_receive(k - 2).astype(BF16))

    slot, row = iota((256, 128), 0), iota((256, 128), 1)
    spread = one_hot((row >> 3 == slot >> 4) & ((row & 7) == (slot & 3)))
    held = (slot & 15) >> 2 == row >> 5
    fold = one_hot(iota((32, 128), 0) == (iota((32, 128), 1) & 31))
    cell_row = ((me - shift_col) & (DEVICES - 1)) * 8 + 4 + twin_col
    received = jnp.zeros((8, 128), F32)
    for quarter, planes in enumerate(QUARTERS):
        groups = [cores[a] * 4 + lax.rem(x - b + 4, 4) for a, b in planes]
        for group in groups:
            got = recv_v.at[pl.ds(pl.multiple_of(group * 16, 16), 16)]
            pltpu.make_async_copy(got, got, recv_sem.at[group]).wait()
        for group in groups:
            sixteen = pl.ds(pl.multiple_of(group * 16, 16), 16)
            lanes = pl.ds(pl.multiple_of(group * 256, 256), 256)
            main = jnp.concatenate(
                [recv_v[sixteen, 16 * h : 16 * h + 16, :].reshape(256, 128) for h in range(2)], axis=1
            )
            layout_out[0:256, lanes] = dot_nt(unit, main).astype(BF16)
            packed = recv_v[sixteen, 32:40, :].astype(F32).reshape(128, 128).astype(BF16)
            wide = jnp.where(held, dot(spread, packed), 0.0).astype(BF16)
            layout_out[256:288, lanes] = dot_nt(fold, wide).astype(BF16)
            received = received + dot(one_hot(iota((8, 128), 1) + group * 128 == cell_row), packed)
        if quarter == 2:
            chosen = ocean_receive(2)
            masked = chosen[8:16] + chosen[0:8] * cell
            atmos_out[...] = jnp.dot(masked, remap, precision=lax.Precision.HIGHEST, preferred_element_type=F32)
    updated_out[...] = anomaly_v[...] + mask_v[...].astype(F32) * received

    sent = send_v.at[pl.ds(0, DEVICES - 1)]
    pltpu.make_async_copy(sent, sent, send_sem).wait()
    for n, (size, _, _, _) in enumerate(steps):
        sent = ahead_recv.at[pl.ds(4 * n, size - 1)]
        pltpu.make_async_copy(sent, sent, ahead_sent.at[n]).wait()


def hand_out(a, b, c, d, a_out, b_out, c_out, d_out, sem):
    pieces = [(b.at[rows], b_out.at[rows]) for rows in (pl.ds(k * 72, 72) for k in range(4))]
    pieces += [(a.at[rows], a_out.at[rows]) for rows in (pl.ds(k * 144, 144) for k in range(2))]
    pieces += [(c, c_out), (d, d_out)]
    copies = [pltpu.make_async_copy(source, result, sem.at[i]) for i, (source, result) in enumerate(pieces)]
    for copy in copies:
        copy.start()
    for copy in copies:
        copy.wait()


def per_device(
    atmosphere_state,
    metric,
    column_group_target,
    physics_input_layer,
    physics_tendency_layer,
    physics_flux_layer,
    block_to_tile,
    remap_weight_matrix,
    ocean_land_mask,
    ocean_sea_anomaly,
    flux_sea_response,
):
    anywhere, vmem, hbm = (pl.BlockSpec(memory_space=space) for space in (pl.ANY, pltpu.VMEM, pltpu.HBM))
    results = [
        jax.ShapeDtypeStruct((WIDTH, COLS), BF16),
        jax.ShapeDtypeStruct((WIDTH, DEVICES * CAP), BF16),
        jax.ShapeDtypeStruct((8, 128), F32),
        jax.ShapeDtypeStruct((8, 128), F32),
    ]
    done = pl.pallas_call(
        kernel,
        out_shape=results,
        in_specs=[hbm] * 12,
        out_specs=[vmem] * 4,
        scratch_shapes=[
            pltpu.VMEM((8, 128), I32),
            pltpu.VMEM((DEVICES, 384), F32),
            pltpu.VMEM((WIDTH, HID), BF16),
            pltpu.VMEM((WIDTH, COLS), BF16),
            pltpu.VMEM((2, COLS), F32),
            pltpu.VMEM((WIDTH + 16, HID), BF16),
            pltpu.VMEM((4, HID), BF16),
            pltpu.VMEM((1, 4), F32),
            pltpu.VMEM((8, 128), I32),
            pltpu.VMEM((8, 128), I32),
            pltpu.VMEM((8, 128), F32),
            pltpu.VMEM((128, 128), F32),
            pltpu.VMEM((HID, WIDTH), BF16),
            pltpu.VMEM((WIDTH, COLS), BF16),
            pltpu.VMEM((HID, COLS), BF16),
            pltpu.VMEM((384, COLS), BF16),
            pltpu.VMEM((8, 128), F32),
            pltpu.VMEM((DEVICES, ROWS, 128), BF16),
            pltpu.VMEM((DEVICES, ROWS, 128), BF16),
            pltpu.VMEM((3, 16, 128), BF16),
            pltpu.VMEM((16, 16, 128), BF16),
            pltpu.SemaphoreType.DMA((15,)),
            pltpu.SemaphoreType.DMA,
            pltpu.SemaphoreType.DMA((8,)),
            pltpu.SemaphoreType.DMA((3,)),
            pltpu.SemaphoreType.DMA((3,)),
        ],
        compiler_params=pltpu.CompilerParams(
            collective_id=0, has_side_effects=True, vmem_limit_bytes=VMEM_LIMIT
        ),
        name="coupling_interval",
    )(*[pltpu.with_memory_space_constraint(v, pltpu.HBM) for v in (
        column_group_target.reshape(DEVICES, 8, 128),
        jnp.asarray(tables()),
        physics_input_layer,
        atmosphere_state.reshape(WIDTH, COLS),
        metric,
        physics_tendency_layer.T,
        physics_flux_layer.T,
        flux_sea_response.reshape(1, 4),
        block_to_tile.reshape(8, 128),
        ocean_land_mask,
        ocean_sea_anomaly,
        remap_weight_matrix,
    )])
    stepped, layout, updated, atmos = pl.pallas_call(
        hand_out,
        out_shape=results,
        in_specs=[anywhere] * 4,
        out_specs=[anywhere] * 4,
        scratch_shapes=[pltpu.SemaphoreType.DMA((8,))],
        compiler_params=pltpu.CompilerParams(vmem_limit_bytes=4 * 1024 * 1024),
        name="hand_out",
    )(*done)
    return (
        stepped.reshape(atmosphere_state.shape),
        layout.T,
        updated,
        atmos.reshape(COLS),
    )


def solution(mesh):
    placed = (
        P(None, None, ("sect", "dev")),
        P(None, ("sect", "dev")),
        P(),
        P(),
        P(),
        P(),
        P(),
        P(),
        P(("sect", "dev"), None),
        P(("sect", "dev"), None),
        P(),
    )
    return jax.shard_map(
        per_device,
        mesh=mesh,
        in_specs=placed,
        out_specs=(
            P(None, None, ("sect", "dev")),
            P(("sect", "dev"), None),
            P(("sect", "dev"), None),
            P(("sect", "dev")),
        ),
        check_vma=False,
    )
```

time: 35.3 us -> 32.7 us (0.926)
  Pallas kernels: 34.5 us -> 31.9 us
    pallas_call x1, Pallas kernels: 33.3 us -> 30.7 us  [per_device(): pl.pallas_call(kernel, out_shape=results, in_specs=[hbm] * 12, out_specs=...]
where the time goes in v3:
time: 32.7 us; the launch traced here: 32.6 us
  Pallas kernels  31.9 us (98%)
  between operations  0.64 us (2%)
    pallas_call x1, Pallas kernels, per_device(): pl.pallas_call(kernel, out_shape=results, in_specs=[hbm] * 12, out_specs=...  30.7 us
    pallas_call x1, Pallas kernels, per_device(): pl.pallas_call(hand_out, out_shape=results, in_specs=[anywhere] * 4, out_...  1.28 us

profile of v3, /device:TPU:1, one launch (start us, length us, event | category | flops | bytes accessed | tf_op | source)
XLA Modules:
  0.0 32.6 jit_solution(709578697350682175)
XLA Ops:
  0.6 30.7 %coupling_interval.1 = (bf16[288,1024]{1,0:T(8,128)(2,1)S(1)}, bf16[288,2048]{1,0:T(8,128)(2,1)S(1)}, f32[8,128]{1,0:T(8,128)S(1)}, f32[8,128]{1,0:T(8,128)S(1)}) custom-call(s32[128,8,128]{2,1,0:T(8,128)} %bitcast.11, f32[128,384]{1,0:T(8,128)} %constant.2.clone.table_hbm, bf16[288,1024]{1,0:T(8,128)(2,1)} %w1_hbm.1, bf16[288,1024]{1,0:T(8,128)(2,1)} %bitcast.9, ...), custom_call_target="tpu_custom_call" | custom-call | tf_op jit(solution)/shard_map/coupling_interval/pallas_call | solution.py:404
  31.3 1.3 %hand_out.1 = (bf16[288,1024]{1,0:T(8,128)(2,1)}, bf16[288,2048]{1,0:T(8,128)(2,1)}, f32[8,128]{1,0:T(8,128)}, f32[8,128]{1,0:T(8,128)}) custom-call(bf16[288,1024]{1,0:T(8,128)(2,1)S(1)} %get-tuple-element.12.a, bf16[288,2048]{1,0:T(8,128)(2,1)S(1)} %get-tuple-element.13.b, f32[8,128]{1,0:T(8,128)S(1)} %get-tuple-element.14.c, f32[8,128]{1,0:T(8,128)S(1)} %get-tuple-element.15.d), custom_call_target="tpu_custom_call" | custom-call | tf_op jit(solution)/shard_map/hand_out/pallas_call | solution.py:455

commit v4 on v3

--- a/solution.py
+++ b/solution.py
@@ -20,9 +20,10 @@
 COLS = 1024
 WIDTH = 288
 HID = 1024
-ROWS = 40
+ROWS = 9
 STEP = 256
 WIDE = 512
+EARLY = 5
 VMEM_LIMIT = 32 * 1024 * 1024
 NT = (((1,), (1,)), ((), ()))
 
@@ -56,7 +57,8 @@
 SELF = (0, 0, 0, 0)
 ORDER = message_order()
 FAR_FIRST = sorted(ORDER, key=lambda o: -sum(min(k, 4 - k) for k in o[1:]))
-CHUNKS = [8, 24, 32, 32, 32]
+DIRECT = [16, 16]
+CHUNKS = [32, 32, 32]
 
 
 def tables():
@@ -122,13 +124,17 @@
     q_v,
     send_v,
     recv_v,
-    ahead_send,
-    ahead_recv,
+    ocean_out,
+    ocean_in,
+    cell_out,
+    cell_in,
     in_sem,
     send_sem,
     recv_sem,
-    ahead_sent,
-    ahead_sem,
+    ocean_sent,
+    ocean_came,
+    cell_sent,
+    cell_came,
 ):
     core, chip = lax.axis_index("sect"), lax.axis_index("dev")
     me = core * 64 + chip
@@ -136,13 +142,13 @@
 
     half = COLS // 2
     pairs = [
+        (target_hbm.at[me], target_v),
+        (table_hbm, table_v),
+        (metric_hbm, metric_v),
         (state_hbm.at[:, pl.ds(0, half)], x_v.at[:, pl.ds(0, half)]),
         (state_hbm.at[:, pl.ds(half, half)], x_v.at[:, pl.ds(half, half)]),
-        (metric_hbm, metric_v),
-        (table_hbm, table_v),
         (w1_hbm.at[:, pl.ds(0, half)], w1_v.at[:, pl.ds(0, half)]),
         (w1_hbm.at[:, pl.ds(half, half)], w1_v.at[:, pl.ds(half, half)]),
-        (target_hbm.at[me], target_v),
         (w2t_hbm.at[:, pl.ds(0, half)], w23_v.at[pl.ds(0, WIDTH), pl.ds(0, half)]),
         (w2t_hbm.at[:, pl.ds(half, half)], w23_v.at[pl.ds(0, WIDTH), pl.ds(half, half)]),
         (w3t_hbm, w3t_v),
@@ -165,7 +171,7 @@
         if (a, b, e, f) != SELF:
             pl.semaphore_signal(barrier, inc=1, device_id=(cores[a], xs[b] + ys[e] + zs[f]), device_id_type=MESH)
 
-    for load in loads[0:4]:
+    for load in loads[0:5]:
         load.wait()
     deriv = table_v[:, 0:256].astype(BF16)
 
@@ -203,29 +209,9 @@
             j = c * (WIDE // 128) + b
             q_v[j : j + 1, :] = mixed[:, b * 128 : (b + 1) * 128]
 
-    for b in range(WIDE // 128):
+    for b in range(COLS // 128):
         dynamics(b)
 
-    for load in loads[4:7]:
-        load.wait()
-    unit = one_hot(iota((256, 256), 0) == iota((256, 256), 1))
-    for b in range(HID // 256):
-        rows = slice(b * 256, (b + 1) * 256)
-        w1t_v[rows, :] = dot_nt(unit, w1_v[:, rows]).astype(BF16)
-
-    for c in range(COLS // WIDE):
-        for b in range(HID // 256):
-            first_layer(c, b)
-            if c + 1 < COLS // WIDE:
-                for d in range(WIDE // 512):
-                    dynamics((c + 1) * WIDE // 128 + b * (WIDE // 512) + d)
-        if c == 0:
-            for load in loads[7:]:
-                load.wait()
-            w3t = w3t_v[...].astype(F32)
-            w23_v[WIDTH : WIDTH + 16, :] = jnp.concatenate([w3t, jnp.zeros((12, HID), F32)], axis=0).astype(BF16)
-        else:
-            second_layer(c - 1)
     order = table_v[:, 256:384].astype(I32)
     to_device = (
         ((order[:, 0:1] + core) & 1) * 64
@@ -248,76 +234,19 @@
         slots.append(jnp.sum(slot, axis=0, keepdims=True))
     slots = jnp.concatenate(slots, axis=1)
 
-    second_layer(COLS // WIDE - 1)
-
-    lane, sub = iota((8, 128), 1), iota((8, 128), 0)
-    shift_row = jnp.where(iota((1, 128), 1) < 8, tile_v[0:1, :] >> 3, -1)
-    shift_col = jnp.sum(jnp.where(lane == sub, shift_row, 0), axis=1, keepdims=True)
-    same = jnp.where((shift_row == shift_col) & (lane < 8), 1, 0)
-    twin_row = jnp.sum(jnp.where(sub < lane, same, 0), axis=0, keepdims=True)
-    twin_col = jnp.sum(jnp.where(lane < sub, same, 0), axis=1, keepdims=True)
-
-    ocean = mask_v[...].astype(F32)
-    ahead = jnp.concatenate([ocean, ocean * anomaly_v[...]], axis=0).astype(BF16)
-    tile_device = (me + jnp.concatenate([shift_col, shift_col], axis=0)) & (DEVICES - 1)
     plane = lax.div(me, 16)
-    steps = [
-        (4, z, tile_device & 3, lambda k: plane * 16 + y * 4 + k),
-        (4, y, (tile_device >> 2) & 3, lambda k: plane * 16 + k * 4 + z),
-        (8, plane, tile_device >> 4, lambda k: k * 16 + y * 4 + z),
-    ]
-
-    def ocean_send(n, rows):
-        size, mine, _, peer = steps[n]
-        ahead_send[n] = rows
-        ahead_recv[4 * n + mine] = rows
-        for k in range(1, size):
-            pltpu.make_async_remote_copy(
-                ahead_send.at[n],
-                ahead_recv.at[4 * n + mine],
-                ahead_sent.at[n],
-                ahead_sem.at[n],
-                device_id=device(peer(lax.rem(mine + k, size))),
-                device_id_type=MESH,
-            ).start()
-
-    def ocean_receive(n):
-        size, _, source, _ = steps[n]
-        got = ahead_recv.at[pl.ds(4 * n, size - 1)]
-        pltpu.make_async_copy(got, got, ahead_sem.at[n]).wait()
-        chosen = jnp.zeros((16, 128), F32)
-        for k in range(size):
-            chosen = chosen + jnp.where(source == k, ahead_recv[4 * n + k].astype(F32), 0.0)
-        return chosen
-
-    remap = remap_v[...]
-    cell = dot_nt(q_v[...], remap, lax.Precision.HIGHEST)
-    cell_rows = jnp.concatenate([cell, jnp.zeros((120, 128), F32)], axis=0).astype(BF16)
-    cell_to = jnp.where(shift_row < 0, -1, (shift_row + me) & (DEVICES - 1))
-    cell_rows = [dot(one_hot((to_device == cell_to) & (twin_row == u)), cell_rows) for u in range(2)]
-
-    pl.semaphore_wait(barrier, DEVICES - 1)
-
-    ocean_send(0, ahead)
-
-    first = 0
-    for k, count in enumerate(CHUNKS):
-        size = count * CAP
-        pick = one_hot(iota((size, COLS), 0) + first * CAP == slots)
-        placed = dot_nt(pick, tend_v[...])
-        into = pl.ds(first, count)
-        main = placed[:, 0:256].astype(BF16)
-        send_v[into, 0:16, :] = main[:, 0:128].reshape(count, CAP, 128)
-        send_v[into, 16:32, :] = main[:, 128:256].reshape(count, CAP, 128)
+
+    def lay_out(first, count, main, tail):
+        size, into = count * CAP, pl.ds(first, count)
+        main = main.astype(BF16)
+        send_v[into, 0:4] = main[:, 0:128].reshape(count, 4, 4, 128)
+        send_v[into, 4:8] = main[:, 128:256].reshape(count, 4, 4, 128)
         keep = (iota((size, 128), 0) & 15) >> 2 == iota((size, 128), 1) >> 5
-        tail = jnp.where(keep, placed[:, 256:384], 0.0).reshape(count, CAP, 128)
+        tail = jnp.where(keep, tail, 0.0).reshape(count, CAP, 128)
         tail = tail[:, 0:8] + tail[:, 8:16]
-        tail = tail + jnp.concatenate([tail[:, 4:8], tail[:, 0:4]], axis=1)
-        packed_row = iota((count, 8, 128), 1)
-        for u in range(2):
-            row = cell_rows[u][first : first + count].reshape(count, 1, 128)
-            tail = jnp.where(packed_row == 4 + u, row, tail)
-        send_v[into, 32:40, :] = tail.astype(BF16)
+        send_v[into, 8] = (tail[:, 0:4] + tail[:, 4:8]).astype(BF16)
+
+    def issue(first, count):
         for i in range(first, first + count):
             a, b, e, f = ORDER[i]
             if ORDER[i] == SELF:
@@ -331,16 +260,113 @@
                 device_id=(cores[a], xs[b] + ys[e] + zs[f]),
                 device_id_type=MESH,
             ).start()
+
+    def pick(first, count):
+        return one_hot(iota((count * CAP, COLS), 0) + first * CAP == slots)
+
+    for load in loads[5:]:
+        load.wait()
+    lane, sub = iota((8, 128), 1), iota((8, 128), 0)
+    shift_row = jnp.where(iota((1, 128), 1) < 8, tile_v[0:1, :] >> 3, -1)
+    shift_col = jnp.sum(jnp.where(lane == sub, shift_row, 0), axis=1, keepdims=True)
+
+    def steps(devices):
+        return [
+            (4, z, devices & 3, lambda k: plane * 16 + y * 4 + k),
+            (4, y, (devices >> 2) & 3, lambda k: plane * 16 + k * 4 + z),
+            (8, plane, devices >> 4, lambda k: k * 16 + y * 4 + z),
+        ]
+
+    def pass_on(way, n, rows):
+        (moves, out_v, in_v, sent, came) = way
+        size, mine, _, peer = moves[n]
+        out_v[n] = rows
+        in_v[4 * n + mine] = rows
+        for k in range(1, size):
+            pltpu.make_async_remote_copy(
+                out_v.at[n],
+                in_v.at[4 * n + mine],
+                sent.at[n],
+                came.at[n],
+                device_id=device(peer(lax.rem(mine + k, size))),
+                device_id_type=MESH,
+            ).start()
+
+    def take(way, n):
+        (moves, _, in_v, _, came) = way
+        size, _, source, _ = moves[n]
+        got = in_v.at[pl.ds(4 * n, size - 1)]
+        pltpu.make_async_copy(got, got, came.at[n]).wait()
+        chosen = jnp.zeros(in_v.shape[1:], F32)
+        for k in range(size):
+            chosen = chosen + jnp.where(source == k, in_v[4 * n + k].astype(F32), 0.0)
+        return chosen
+
+    tile_device = (me + jnp.concatenate([shift_col, shift_col], axis=0)) & (DEVICES - 1)
+    block_device = (me - shift_col) & (DEVICES - 1)
+    to_block = (steps(tile_device), ocean_out, ocean_in, ocean_sent, ocean_came)
+    to_tile = (steps(block_device), cell_out, cell_in, cell_sent, cell_came)
+    ocean = mask_v[...].astype(F32)
+    ahead = jnp.concatenate([ocean, ocean * anomaly_v[...]], axis=0).astype(BF16)
+
+    w2_tail = jnp.concatenate([w23_v[256:288, :]] * 4, axis=0)
+    late = x + y + z >= EARLY
+    first = 0
+    for count in DIRECT:
+        field = dot_nt(pick(first, count), adv_v[...]).astype(BF16)
+        half = 0.5 * dot(field, w1_v[...])
+        hidden = (half + half * jnp.tanh(half)).astype(BF16)
+        main, tail = dot_nt(hidden, w23_v[0:256, :]), dot_nt(hidden, w2_tail)
+        lay_out(first, count, main, tail)
+
+        @pl.when(late)
+        def _():
+            if first == 0:
+                pl.semaphore_wait(barrier, DEVICES - 1)
+                pass_on(to_block, 0, ahead)
+            issue(first, count)
+
         first += count
-        if k in (2, 3):
-            ocean_send(k - 1, ocean_receive(k - 2).astype(BF16))
-
-    slot, row = iota((256, 128), 0), iota((256, 128), 1)
-    spread = one_hot((row >> 3 == slot >> 4) & ((row & 7) == (slot & 3)))
-    held = (slot & 15) >> 2 == row >> 5
+
+    unit = one_hot(iota((256, 256), 0) == iota((256, 256), 1))
+    for b in range(HID // 256):
+        rows = slice(b * 256, (b + 1) * 256)
+        w1t_v[rows, :] = dot_nt(unit, w1_v[:, rows]).astype(BF16)
+
+    w3t = w3t_v[...].astype(F32)
+    w23_v[WIDTH : WIDTH + 16, :] = jnp.concatenate([w3t, jnp.zeros((12, HID), F32)], axis=0).astype(BF16)
+    for c in range(COLS // WIDE):
+        for b in range(HID // 256):
+            first_layer(c, b)
+        if c > 0:
+            second_layer(c - 1)
+    second_layer(COLS // WIDE - 1)
+
+    remap = remap_v[...]
+    cell = dot_nt(q_v[...], remap, lax.Precision.HIGHEST)
+
+    @pl.when(jnp.logical_not(late))
+    def _():
+        pl.semaphore_wait(barrier, DEVICES - 1)
+        pass_on(to_block, 0, ahead)
+        issue(0, sum(DIRECT))
+
+    pass_on(to_tile, 0, cell)
+
+    for n, count in enumerate(CHUNKS):
+        placed = dot_nt(pick(first, count), tend_v[...])
+        lay_out(first, count, placed[:, 0:256], placed[:, 256:384])
+        issue(first, count)
+        first += count
+        if n < 2:
+            pass_on(to_block, n + 1, take(to_block, n).astype(BF16))
+        if n > 0:
+            pass_on(to_tile, n, take(to_tile, n - 1))
+
+    slot, row = iota((256, 64), 0), iota((256, 64), 1)
+    spread = one_hot((row >> 2 == slot >> 4) & ((row & 3) == (slot & 3)))
+    held = (iota((256, 128), 0) & 15) >> 2 == iota((256, 128), 1) >> 5
     fold = one_hot(iota((32, 128), 0) == (iota((32, 128), 1) & 31))
-    cell_row = ((me - shift_col) & (DEVICES - 1)) * 8 + 4 + twin_col
-    received = jnp.zeros((8, 128), F32)
     for quarter, planes in enumerate(QUARTERS):
         groups = [cores[a] * 4 + lax.rem(x - b + 4, 4) for a, b in planes]
         for group in groups:
@@ -349,25 +375,23 @@
         for group in groups:
             sixteen = pl.ds(pl.multiple_of(group * 16, 16), 16)
             lanes = pl.ds(pl.multiple_of(group * 256, 256), 256)
-            main = jnp.concatenate(
-                [recv_v[sixteen, 16 * h : 16 * h + 16, :].reshape(256, 128) for h in range(2)], axis=1
-            )
+            main = jnp.concatenate([recv_v[sixteen, h : h + 4].reshape(256, 128) for h in (0, 4)], axis=1)
             layout_out[0:256, lanes] = dot_nt(unit, main).astype(BF16)
-            packed = recv_v[sixteen, 32:40, :].astype(F32).reshape(128, 128).astype(BF16)
-            wide = jnp.where(held, dot(spread, packed), 0.0).astype(BF16)
+            wide = jnp.where(held, dot(spread, recv_v[sixteen, 8].reshape(64, 128)), 0.0).astype(BF16)
             layout_out[256:288, lanes] = dot_nt(fold, wide).astype(BF16)
-            received = received + dot(one_hot(iota((8, 128), 1) + group * 128 == cell_row), packed)
+        if quarter == 1:
+            ahead = take(to_block, 2)
+            masked = ahead[8:16] + ahead[0:8] * cell
+            atmos_out[...] = jnp.dot(masked, remap, precision=lax.Precision.HIGHEST, preferred_element_type=F32)
         if quarter == 2:
-            chosen = ocean_receive(2)
-            masked = chosen[8:16] + chosen[0:8] * cell
-            atmos_out[...] = jnp.dot(masked, remap, precision=lax.Precision.HIGHEST, preferred_element_type=F32)
-    updated_out[...] = anomaly_v[...] + mask_v[...].astype(F32) * received
+            updated_out[...] = anomaly_v[...] + ocean * take(to_tile, 2)
 
     sent = send_v.at[pl.ds(0, DEVICES - 1)]
     pltpu.make_async_copy(sent, sent, send_sem).wait()
-    for n, (size, _, _, _) in enumerate(steps):
-        sent = ahead_recv.at[pl.ds(4 * n, size - 1)]
-        pltpu.make_async_copy(sent, sent, ahead_sent.at[n]).wait()
+    for moves, _, in_v, gone, _ in (to_block, to_tile):
+        for n, (size, _, _, _) in enumerate(moves):
+            sent = in_v.at[pl.ds(4 * n, size - 1)]
+            pltpu.make_async_copy(sent, sent, gone.at[n]).wait()
 
 
 def hand_out(a, b, c, d, a_out, b_out, c_out, d_out, sem):
@@ -424,13 +448,17 @@
             pltpu.VMEM((HID, COLS), BF16),
             pltpu.VMEM((384, COLS), BF16),
             pltpu.VMEM((8, 128), F32),
-            pltpu.VMEM((DEVICES, ROWS, 128), BF16),
-            pltpu.VMEM((DEVICES, ROWS, 128), BF16),
+            pltpu.VMEM((DEVICES, ROWS, 4, 128), BF16),
+            pltpu.VMEM((DEVICES, ROWS, 4, 128), BF16),
             pltpu.VMEM((3, 16, 128), BF16),
             pltpu.VMEM((16, 16, 128), BF16),
+            pltpu.VMEM((3, 8, 128), F32),
+            pltpu.VMEM((16, 8, 128), F32),
             pltpu.SemaphoreType.DMA((15,)),
             pltpu.SemaphoreType.DMA,
             pltpu.SemaphoreType.DMA((8,)),
+            pltpu.SemaphoreType.DMA((3,)),
+            pltpu.SemaphoreType.DMA((3,)),
             pltpu.SemaphoreType.DMA((3,)),
             pltpu.SemaphoreType.DMA((3,)),
         ],

time: 32.7 us -> 31.3 us (0.957)
  Pallas kernels: 31.9 us -> 30.5 us
    pallas_call x1, Pallas kernels: 30.7 us -> 29.2 us  [per_device(): pl.pallas_call(kernel, out_shape=results, in_specs=[hbm] * 12, out_specs=...]
where the time goes in v4:
time: 31.3 us; the launch traced here: 31.1 us
  Pallas kernels  30.5 us (97%)
  between operations  0.64 us (2%)
    pallas_call x1, Pallas kernels, per_device(): pl.pallas_call(kernel, out_shape=results, in_specs=[hbm] * 12, out_specs=...  29.2 us
    pallas_call x1, Pallas kernels, per_device(): pl.pallas_call(hand_out, out_shape=results, in_specs=[anywhere] * 4, out_...  1.28 us

profile of v4, /device:TPU:1, one launch (start us, length us, event | category | flops | bytes accessed | tf_op | source)
XLA Modules:
  0.0 31.1 jit_solution(15189820893041814314)
XLA Ops:
  0.6 29.2 %coupling_interval.1 = (bf16[288,1024]{1,0:T(8,128)(2,1)S(1)}, bf16[288,2048]{1,0:T(8,128)(2,1)S(1)}, f32[8,128]{1,0:T(8,128)S(1)}, f32[8,128]{1,0:T(8,128)S(1)}) custom-call(s32[128,8,128]{2,1,0:T(8,128)} %bitcast.11, f32[128,384]{1,0:T(8,128)} %constant.2.clone.table_hbm, bf16[288,1024]{1,0:T(8,128)(2,1)} %w1_hbm.1, bf16[288,1024]{1,0:T(8,128)(2,1)} %bitcast.9, ...), custom_call_target="tpu_custom_call" | custom-call | tf_op jit(solution)/shard_map/coupling_interval/pallas_call | solution.py:428
  29.9 1.3 %hand_out.1 = (bf16[288,1024]{1,0:T(8,128)(2,1)}, bf16[288,2048]{1,0:T(8,128)(2,1)}, f32[8,128]{1,0:T(8,128)}, f32[8,128]{1,0:T(8,128)}) custom-call(bf16[288,1024]{1,0:T(8,128)(2,1)S(1)} %get-tuple-element.12.a, bf16[288,2048]{1,0:T(8,128)(2,1)S(1)} %get-tuple-element.13.b, f32[8,128]{1,0:T(8,128)S(1)} %get-tuple-element.14.c, f32[8,128]{1,0:T(8,128)S(1)} %get-tuple-element.15.d), custom_call_target="tpu_custom_call" | custom-call | tf_op jit(solution)/shard_map/hand_out/pallas_call | solution.py:483

commit v5 on v4

--- a/solution.py
+++ b/solution.py
@@ -40,7 +40,7 @@
     return np.concatenate([first_dir, second_dir], axis=1)
 
 
-QUARTERS = [[(0, 1), (0, 3)], [(1, 1), (1, 3)], [(0, 2), (0, 0)], [(1, 2), (1, 0)]]
+QUARTERS = [[(0, 1), (0, 3)], [(1, 1), (1, 3)], [(0, 2), (1, 2), (1, 0)], [(0, 0)]]
 
 
 def message_order():

time: 31.3 us -> 30.3 us (0.968)
  Pallas kernels: 30.5 us -> 29.6 us
    pallas_call x1, Pallas kernels: 29.2 us -> 28.3 us  [per_device(): pl.pallas_call(kernel, out_shape=results, in_specs=[hbm] * 12, out_specs=...]
where the time goes in v5:
time: 30.3 us; the launch traced here: 30.2 us
  Pallas kernels  29.6 us (98%)
  between operations  0.64 us (2%)
    pallas_call x1, Pallas kernels, per_device(): pl.pallas_call(kernel, out_shape=results, in_specs=[hbm] * 12, out_specs=...  28.3 us
    pallas_call x1, Pallas kernels, per_device(): pl.pallas_call(hand_out, out_shape=results, in_specs=[anywhere] * 4, out_...  1.28 us

profile of v5, /device:TPU:1, one launch (start us, length us, event | category | flops | bytes accessed | tf_op | source)
XLA Modules:
  0.0 30.2 jit_solution(12029776333880904798)
XLA Ops:
  0.6 28.3 %coupling_interval.1 = (bf16[288,1024]{1,0:T(8,128)(2,1)S(1)}, bf16[288,2048]{1,0:T(8,128)(2,1)S(1)}, f32[8,128]{1,0:T(8,128)S(1)}, f32[8,128]{1,0:T(8,128)S(1)}) custom-call(s32[128,8,128]{2,1,0:T(8,128)} %bitcast.11, f32[128,384]{1,0:T(8,128)} %constant.2.clone.table_hbm, bf16[288,1024]{1,0:T(8,128)(2,1)} %w1_hbm.1, bf16[288,1024]{1,0:T(8,128)(2,1)} %bitcast.9, ...), custom_call_target="tpu_custom_call" | custom-call | tf_op jit(solution)/shard_map/coupling_interval/pallas_call | solution.py:428
  28.9 1.3 %hand_out.1 = (bf16[288,1024]{1,0:T(8,128)(2,1)}, bf16[288,2048]{1,0:T(8,128)(2,1)}, f32[8,128]{1,0:T(8,128)}, f32[8,128]{1,0:T(8,128)}) custom-call(bf16[288,1024]{1,0:T(8,128)(2,1)S(1)} %get-tuple-element.12.a, bf16[288,2048]{1,0:T(8,128)(2,1)S(1)} %get-tuple-element.13.b, f32[8,128]{1,0:T(8,128)S(1)} %get-tuple-element.14.c, f32[8,128]{1,0:T(8,128)S(1)} %get-tuple-element.15.d), custom_call_target="tpu_custom_call" | custom-call | tf_op jit(solution)/shard_map/hand_out/pallas_call | solution.py:483

commit v6 on v5

--- a/solution.py
+++ b/solution.py
@@ -86,6 +86,18 @@
 
 def one_hot(condition):
     return jnp.where(condition, 1.0, 0.0).astype(BF16)
+
+
+def unpack(messages, lanes_out):
+    unit = one_hot(iota((256, 256), 0) == iota((256, 256), 1))
+    slot, row = iota((256, 64), 0), iota((256, 64), 1)
+    spread = one_hot((row >> 2 == slot >> 4) & ((row & 3) == (slot & 3)))
+    held = (iota((256, 128), 0) & 15) >> 2 == iota((256, 128), 1) >> 5
+    fold = one_hot(iota((32, 128), 0) == (iota((32, 128), 1) & 31))
+    main = jnp.concatenate([messages[:, h : h + 4].reshape(256, 128) for h in (0, 4)], axis=1)
+    lanes_out[0:256, :] = dot_nt(unit, main).astype(BF16)
+    wide = jnp.where(held, dot(spread, messages[:, 8].reshape(64, 128)), 0.0).astype(BF16)
+    lanes_out[256:288, :] = dot_nt(fold, wide).astype(BF16)
 
 
 def kernel(
@@ -105,6 +117,7 @@
     layout_out,
     updated_out,
     atmos_out,
+    own_out,
     target_v,
     table_v,
     w1_v,
@@ -363,10 +376,6 @@
         if n > 0:
             pass_on(to_tile, n, take(to_tile, n - 1))
 
-    slot, row = iota((256, 64), 0), iota((256, 64), 1)
-    spread = one_hot((row >> 2 == slot >> 4) & ((row & 3) == (slot & 3)))
-    held = (iota((256, 128), 0) & 15) >> 2 == iota((256, 128), 1) >> 5
-    fold = one_hot(iota((32, 128), 0) == (iota((32, 128), 1) & 31))
     for quarter, planes in enumerate(QUARTERS):
         groups = [cores[a] * 4 + lax.rem(x - b + 4, 4) for a, b in planes]
         for group in groups:
@@ -374,11 +383,11 @@
             pltpu.make_async_copy(got, got, recv_sem.at[group]).wait()
         for group in groups:
             sixteen = pl.ds(pl.multiple_of(group * 16, 16), 16)
+            if quarter == len(QUARTERS) - 1:
+                own_out[...] = recv_v[sixteen]
+                continue
             lanes = pl.ds(pl.multiple_of(group * 256, 256), 256)
-            main = jnp.concatenate([recv_v[sixteen, h : h + 4].reshape(256, 128) for h in (0, 4)], axis=1)
-            layout_out[0:256, lanes] = dot_nt(unit, main).astype(BF16)
-            wide = jnp.where(held, dot(spread, recv_v[sixteen, 8].reshape(64, 128)), 0.0).astype(BF16)
-            layout_out[256:288, lanes] = dot_nt(fold, wide).astype(BF16)
+            unpack(recv_v.at[sixteen], layout_out.at[:, lanes])
         if quarter == 1:
             ahead = take(to_block, 2)
             masked = ahead[8:16] + ahead[0:8] * cell
@@ -394,13 +403,20 @@
             pltpu.make_async_copy(sent, sent, gone.at[n]).wait()
 
 
-def hand_out(a, b, c, d, a_out, b_out, c_out, d_out, sem):
-    pieces = [(b.at[rows], b_out.at[rows]) for rows in (pl.ds(k * 72, 72) for k in range(4))]
-    pieces += [(a.at[rows], a_out.at[rows]) for rows in (pl.ds(k * 144, 144) for k in range(2))]
-    pieces += [(c, c_out), (d, d_out)]
+def hand_out(a, b, c, d, own, a_out, b_out, c_out, d_out, own_v, sem):
+    plane = lax.axis_index("sect") * 4 + lax.div(lax.axis_index("dev"), 16)
+    pieces = []
+    for k in range(1, 8):
+        lanes = pl.ds(pl.multiple_of(lax.rem(plane + k, 8) * 256, 256), 256)
+        pieces.append((b.at[:, lanes], b_out.at[:, lanes]))
+    pieces += [(a, a_out), (c, c_out), (d, d_out)]
     copies = [pltpu.make_async_copy(source, result, sem.at[i]) for i, (source, result) in enumerate(pieces)]
     for copy in copies:
         copy.start()
+    unpack(own, own_v)
+    lanes = pl.ds(pl.multiple_of(plane * 256, 256), 256)
+    copies.append(pltpu.make_async_copy(own_v, b_out.at[:, lanes], sem.at[len(pieces)]))
+    copies[-1].start()
     for copy in copies:
         copy.wait()
 
@@ -427,9 +443,9 @@
     ]
     done = pl.pallas_call(
         kernel,
-        out_shape=results,
+        out_shape=results + [jax.ShapeDtypeStruct((16, ROWS, 4, 128), BF16)],
         in_specs=[hbm] * 12,
-        out_specs=[vmem] * 4,
+        out_specs=[vmem] * 5,
         scratch_shapes=[
             pltpu.VMEM((8, 128), I32),
             pltpu.VMEM((DEVICES, 384), F32),
@@ -483,9 +499,9 @@
     stepped, layout, updated, atmos = pl.pallas_call(
         hand_out,
         out_shape=results,
-        in_specs=[anywhere] * 4,
+        in_specs=[anywhere] * 4 + [vmem],
         out_specs=[anywhere] * 4,
-        scratch_shapes=[pltpu.SemaphoreType.DMA((8,))],
+        scratch_shapes=[pltpu.VMEM((WIDTH, 256), BF16), pltpu.SemaphoreType.DMA((11,))],
         compiler_params=pltpu.CompilerParams(vmem_limit_bytes=4 * 1024 * 1024),
         name="hand_out",
     )(*done)

time: 30.3 us -> 30.1 us (level)
  no operation moved by 1% of the time
where the time goes in v6:
time: 30.1 us; the launch traced here: 30 us
  Pallas kernels  29.3 us (97%)
  between operations  0.64 us (2%)
    pallas_call x1, Pallas kernels, per_device(): pl.pallas_call(kernel, out_shape=results + [jax.ShapeDtypeStruct((16, ROW...  28 us
    pallas_call x1, Pallas kernels, per_device(): pl.pallas_call(hand_out, out_shape=results, in_specs=[anywhere] * 4 + [vm...  1.34 us

profile of v6, /device:TPU:1, one launch (start us, length us, event | category | flops | bytes accessed | tf_op | source)
XLA Modules:
  0.0 30.0 jit_solution(11594783442236986486)
XLA Ops:
  0.6 28.0 %coupling_interval.1 = (bf16[288,1024]{1,0:T(8,128)(2,1)S(1)}, bf16[288,2048]{1,0:T(8,128)(2,1)S(1)}, f32[8,128]{1,0:T(8,128)S(1)}, f32[8,128]{1,0:T(8,128)S(1)}, bf16[16,9,4,128]{3,2,1,0:T(4,128)(2,1)S(1)}) custom-call(s32[128,8,128]{2,1,0:T(8,128)} %bitcast.11, f32[128,384]{1,0:T(8,128)} %constant.2.clone.table_hbm, bf16[288,1024]{1,0:T(8,128)(2,1)} %w1_hbm.1, ...), custom_call_target="tpu_custom_call" | custom-call | tf_op jit(solution)/shard_map/coupling_interval/pallas_call | solution.py:444
  28.6 1.3 %hand_out.1 = (bf16[288,1024]{1,0:T(8,128)(2,1)}, bf16[288,2048]{1,0:T(8,128)(2,1)}, f32[8,128]{1,0:T(8,128)}, f32[8,128]{1,0:T(8,128)}) custom-call(bf16[288,1024]{1,0:T(8,128)(2,1)S(1)} %get-tuple-element.13.a, bf16[288,2048]{1,0:T(8,128)(2,1)S(1)} %get-tuple-element.14.b, f32[8,128]{1,0:T(8,128)S(1)} %get-tuple-element.15.c, ...), custom_call_target="tpu_custom_call" | custom-call | tf_op jit(solution)/shard_map/hand_out/pallas_call | solution.py:499

commit v7 on v6

--- a/solution.py
+++ b/solution.py
@@ -41,6 +41,7 @@
 
 
 QUARTERS = [[(0, 1), (0, 3)], [(1, 1), (1, 3)], [(0, 2), (1, 2), (1, 0)], [(0, 0)]]
+ARRIVALS = [[(0, 1), (0, 3)], [(1, 1), (1, 3)], [(0, 2), (1, 2)], [(1, 0), (0, 0)]]
 
 
 def message_order():
@@ -376,15 +377,15 @@
         if n > 0:
             pass_on(to_tile, n, take(to_tile, n - 1))
 
-    for quarter, planes in enumerate(QUARTERS):
+    for quarter, planes in enumerate(ARRIVALS):
         groups = [cores[a] * 4 + lax.rem(x - b + 4, 4) for a, b in planes]
         for group in groups:
             got = recv_v.at[pl.ds(pl.multiple_of(group * 16, 16), 16)]
             pltpu.make_async_copy(got, got, recv_sem.at[group]).wait()
-        for group in groups:
+        for k, group in enumerate(groups):
             sixteen = pl.ds(pl.multiple_of(group * 16, 16), 16)
-            if quarter == len(QUARTERS) - 1:
-                own_out[...] = recv_v[sixteen]
+            if quarter == len(ARRIVALS) - 1:
+                own_out[16 * k : 16 * k + 16] = recv_v[sixteen]
                 continue
             lanes = pl.ds(pl.multiple_of(group * 256, 256), 256)
             unpack(recv_v.at[sixteen], layout_out.at[:, lanes])
@@ -406,17 +407,18 @@
 def hand_out(a, b, c, d, own, a_out, b_out, c_out, d_out, own_v, sem):
     plane = lax.axis_index("sect") * 4 + lax.div(lax.axis_index("dev"), 16)
     pieces = []
-    for k in range(1, 8):
+    for k in (1, 2, 3, 5, 6, 7):
         lanes = pl.ds(pl.multiple_of(lax.rem(plane + k, 8) * 256, 256), 256)
         pieces.append((b.at[:, lanes], b_out.at[:, lanes]))
     pieces += [(a, a_out), (c, c_out), (d, d_out)]
     copies = [pltpu.make_async_copy(source, result, sem.at[i]) for i, (source, result) in enumerate(pieces)]
     for copy in copies:
         copy.start()
-    unpack(own, own_v)
-    lanes = pl.ds(pl.multiple_of(plane * 256, 256), 256)
-    copies.append(pltpu.make_async_copy(own_v, b_out.at[:, lanes], sem.at[len(pieces)]))
-    copies[-1].start()
+    for k in range(2):
+        unpack(own.at[pl.ds(16 * k, 16)], own_v.at[k])
+        lanes = pl.ds(pl.multiple_of(lax.rem(plane + 4 - 4 * k, 8) * 256, 256), 256)
+        copies.append(pltpu.make_async_copy(own_v.at[k], b_out.at[:, lanes], sem.at[len(copies)]))
+        copies[-1].start()
     for copy in copies:
         copy.wait()
 
@@ -443,7 +445,7 @@
     ]
     done = pl.pallas_call(
         kernel,
-        out_shape=results + [jax.ShapeDtypeStruct((16, ROWS, 4, 128), BF16)],
+        out_shape=results + [jax.ShapeDtypeStruct((32, ROWS, 4, 128), BF16)],
         in_specs=[hbm] * 12,
         out_specs=[vmem] * 5,
         scratch_shapes=[
@@ -501,7 +503,7 @@
         out_shape=results,
         in_specs=[anywhere] * 4 + [vmem],
         out_specs=[anywhere] * 4,
-        scratch_shapes=[pltpu.VMEM((WIDTH, 256), BF16), pltpu.SemaphoreType.DMA((11,))],
+        scratch_shapes=[pltpu.VMEM((2, WIDTH, 256), BF16), pltpu.SemaphoreType.DMA((11,))],
         compiler_params=pltpu.CompilerParams(vmem_limit_bytes=4 * 1024 * 1024),
         name="hand_out",
     )(*done)

time: 30.1 us -> 30.4 us (level)
  no operation moved by 1% of the time
where the time goes in v7:
time: 30.4 us; the launch traced here: 30.2 us
  Pallas kernels  29.6 us (97%)
  between operations  0.64 us (2%)
    pallas_call x1, Pallas kernels, per_device(): pl.pallas_call(kernel, out_shape=results + [jax.ShapeDtypeStruct((32, ROW...  28 us
    pallas_call x1, Pallas kernels, per_device(): pl.pallas_call(hand_out, out_shape=results, in_specs=[anywhere] * 4 + [vm...  1.56 us

profile of v7, /device:TPU:1, one launch (start us, length us, event | category | flops | bytes accessed | tf_op | source)
XLA Modules:
  0.0 30.2 jit_solution(7824869572488960701)
XLA Ops:
  0.6 28.0 %coupling_interval.1 = (bf16[288,1024]{1,0:T(8,128)(2,1)S(1)}, bf16[288,2048]{1,0:T(8,128)(2,1)S(1)}, f32[8,128]{1,0:T(8,128)S(1)}, f32[8,128]{1,0:T(8,128)S(1)}, bf16[32,9,4,128]{3,2,1,0:T(4,128)(2,1)S(1)}) custom-call(s32[128,8,128]{2,1,0:T(8,128)} %bitcast.11, f32[128,384]{1,0:T(8,128)} %constant.2.clone.table_hbm, bf16[288,1024]{1,0:T(8,128)(2,1)} %w1_hbm.1, ...), custom_call_target="tpu_custom_call" | custom-call | tf_op jit(solution)/shard_map/coupling_interval/pallas_call | solution.py:446
  28.7 1.6 %hand_out.1 = (bf16[288,1024]{1,0:T(8,128)(2,1)}, bf16[288,2048]{1,0:T(8,128)(2,1)}, f32[8,128]{1,0:T(8,128)}, f32[8,128]{1,0:T(8,128)}) custom-call(bf16[288,1024]{1,0:T(8,128)(2,1)S(1)} %get-tuple-element.13.a, bf16[288,2048]{1,0:T(8,128)(2,1)S(1)} %get-tuple-element.14.b, f32[8,128]{1,0:T(8,128)S(1)} %get-tuple-element.15.c, ...), custom_call_target="tpu_custom_call" | custom-call | tf_op jit(solution)/shard_map/hand_out/pallas_call | solution.py:501
